TPU v7x, 256 devices: a whole 4x4x8 slice. The times are simulated.
256 devices in a mesh: seq: 8 (over y, x_hi), dp: 32 (over z, x_lo, core).
Axes of the slice: x: 4 (x_hi: 2, x_lo: 2; x = x_hi * 2 + x_lo), y: 4, z: 8, core: 2. Of those that a mesh axis runs over, the one named last changes fastest.
Arguments:
- input_tokens: bfloat16 [32, 1024, 5120], P('dp', 'seq'), may hold values from -6 to 6
- query_unnormed: bfloat16 [32, 1024, 3072], P('dp', 'seq'), may hold values from -6 to 6
- key_unnormed: bfloat16 [32, 1024, 3072], P('dp', 'seq'), may hold values from -6 to 6
- value_projected: bfloat16 [32, 1024, 3072], P('dp', 'seq'), may hold values from -6 to 6
- cotangent: bfloat16 [32, 1024, 3072], P('dp', 'seq'), may hold values from -0.625 to 0.625
- query_norm_gain: float32 [3072], replicated, may hold values from 0.5 to 1.5
- key_norm_gain: float32 [3072], replicated, may hold values from 0.5 to 1.5
- adapter_down_maps: bfloat16 [3, 32, 5120], replicated, may hold values from -0.078125 to 0.078125
- adapter_up_maps: bfloat16 [3, 32, 3072], replicated, may hold values from -0.109375 to 0.109375
- generated_mask: int32 [32, 8, 128], P('dp', 'seq'), may hold values 0 or 1
- block_begin_flags: int32 [32, 8], P('dp'), may hold values from 0 to 1, as said below
Outputs:
- grad_down: bfloat16 [3, 32, 5120], replicated
- grad_up: bfloat16 [3, 32, 3072], replicated
Inputs may be any that keep to these rules, and one draw needn't show every extreme that they name: `block_begin_flags`: the first frame of every video begins a causal block.
All inputs are finite; a program needn't handle non-finite values. No bound on the sum of `generated_mask` on one device may be relied on, other than what follows from the above.
Results may differ from a plain program's by a relative error of at most 0.01025.
The roundings to bfloat16 on the way count: a program that leaves them out, or rounds other values in their place, can miss the bound.
Values may be sent and summed in bfloat16 or wider, within the bound.
No kernel may reach another device: no remote copies, remote signals or barrier semaphores. Data moves between devices by JAX's collectives and lax.ppermute only.
A program may use at most 128 MiB of HBM per device.

v0:
```python
import functools
import math

import jax
import jax.numpy as jnp
import numpy as np
from jax import lax
from jax.experimental import pallas as pl
from jax.experimental.pallas import tpu as pltpu
from jax.sharding import PartitionSpec as P

HEADS = 24
HEAD_DIM = 128
GRID_W = 16
FRAME_TOK = 128
FRAMES = 8
RANK = 32
WIDTH = 5120
CHANNELS = 3072
GROUPS = 8
LOCAL_HEADS = 3
NORM_EPS = 1e-06
SCALING = 1.0 / math.sqrt(HEAD_DIM)
BF = jnp.bfloat16
F32 = jnp.float32
HIDDEN = -1e30
BIG = 58
COLS = WIDTH // 8
GCOLS = CHANNELS // 8
BOTH = COLS + GCOLS

VMEM = pl.BlockSpec(memory_space=pltpu.VMEM)
SMEM = pl.BlockSpec(memory_space=pltpu.SMEM)


def params(mib):
    return pltpu.CompilerParams(vmem_limit_bytes=mib * 1024 * 1024)


def rope_tables():
    time_dims = HEAD_DIM - 4 * (HEAD_DIM // 6)
    space_dims = 2 * (HEAD_DIM // 6)
    tp, sp = time_dims // 2, space_dims // 2
    tok = np.arange(FRAMES * FRAME_TOK)
    frame, within = tok // FRAME_TOK, tok % FRAME_TOK
    row, col = within // GRID_W, within % GRID_W
    pairs = np.arange(HEAD_DIM) // 2
    in_time = pairs < tp
    in_rows = (pairs >= tp) & (pairs < tp + sp)
    offset = np.where(in_time, pairs, np.where(in_rows, pairs - tp, pairs - tp - sp))
    extent = np.where(in_time, time_dims, space_dims)
    rates = np.exp(-math.log(10000.0) * (2 * offset) / extent)
    pos = np.where(
        in_time[None], frame[:, None], np.where(in_rows[None], row[:, None], col[:, None])
    )
    angle = pos * rates[None]
    even = (np.arange(HEAD_DIM) % 2 == 0)[None]
    sine = np.sin(angle)
    table = np.stack([np.cos(angle), np.where(even, -sine, 0.0), np.where(even, 0.0, sine)], 0)
    table = table.reshape(3, FRAMES, FRAME_TOK, HEAD_DIM)
    by_frame = np.where(in_time[None, None], table[:, :, 0], 0.0).transpose(1, 0, 2)
    within = np.where(in_time[None, None], 0.0, table[:, 0])
    return by_frame.reshape(3 * FRAMES, HEAD_DIM).astype(np.float32), within.astype(np.float32)


def turn(z, by_frame, within, frame, sign):
    cosine, left, right = (
        within[n] + by_frame[pl.ds(3 * frame + n, 1), :] for n in range(3)
    )
    mixed = pltpu.roll(z, HEAD_DIM - 1, 1) * left + pltpu.roll(z, 1, 1) * right
    base = z * cosine
    return base + mixed if sign > 0 else base - mixed


def position():
    s, d = lax.axis_index("seq"), lax.axis_index("dp")
    x = lax.rem(s, 2) * 2 + lax.rem(lax.div(d, 2), 2)
    return s, lax.div(s, 2), x, lax.rem(d, 2)


def nt(a, b, **kw):
    return lax.dot_general(
        a, b, (((1,), (1,)), ((), ())), preferred_element_type=F32, **kw
    )


def nn(a, b):
    return lax.dot_general(a, b, (((1,), (0,)), ((), ())), preferred_element_type=F32)


def rho_of(raw):
    total = jnp.zeros((raw.shape[0], HEAD_DIM), F32)
    for n in range(HEADS):
        part = raw[:, n * HEAD_DIM : (n + 1) * HEAD_DIM].astype(F32)
        total = total + part * part
    mean = jnp.sum(total, axis=1, keepdims=True) * (1.0 / CHANNELS)
    return lax.rsqrt(mean + NORM_EPS)


def pack_kernel(heads, query, key, value, cot, mask, gain_q, gain_k, by_frame, within, *refs):
    s = lax.axis_index("seq")
    ups, downs, tokens, outs, local, keep_s = refs if len(refs) > 2 else (None,) * 3 + (refs[0], None, refs[1])
    count = query.shape[0]
    keep_s[...] = jnp.broadcast_to(mask[...].astype(F32), (FRAME_TOK, FRAME_TOK)).T
    keep = keep_s[pl.ds(pl.multiple_of(pl.program_id(0) * count, count), count), :] > 0.0
    rhos = [rho_of(raw) for raw in (query, key)]
    for k in range(GROUPS):
        for i, h in enumerate(heads):
            head = k * LOCAL_HEADS + h
            at = slice(head * HEAD_DIM, (head + 1) * HEAD_DIM)
            for n, (raw, gain) in enumerate(((query, gain_q), (key, gain_k))):
                normed = raw[:, at].astype(F32) * rhos[n] * gain[head : head + 1, :]
                outs[k, 4 * i + n] = turn(normed, by_frame, within, s, 1).astype(BF)
            outs[k, 4 * i + 2] = value[:, at]
            outs[k, 4 * i + 3] = jnp.where(keep, cot[:, at].astype(F32), 0.0).astype(BF)
    if ups is None:
        return
    rows = []
    for n, raw in ((0, query), (1, key)):
        rows.append(jnp.broadcast_to(rhos[n], (FRAME_TOK, FRAME_TOK)).T[0:8])
        carried = jnp.zeros((RANK, FRAME_TOK), F32)
        for head in range(HEADS):
            at = slice(head * HEAD_DIM, (head + 1) * HEAD_DIM)
            normed = (raw[:, at].astype(F32) * rhos[n]).astype(BF)
            carried = carried + nt(ups[n, :, at], normed)
        local[n * RANK : (n + 1) * RANK, :] = carried
        local[64 + 8 * n : 72 + 8 * n, :] = rows[n]
    down = nt(downs[...], tokens[...])
    at_row = lax.broadcasted_iota(jnp.int32, (RANK, FRAME_TOK), 0)
    extra = jnp.zeros((RANK, FRAME_TOK), F32)
    for n in range(2):
        wide = jnp.concatenate([rows[n]] * 4, 0)
        high = wide.astype(BF).astype(F32)
        extra = jnp.where(at_row == 2 * n, high, extra)
        extra = jnp.where(at_row == 2 * n + 1, wide - high, extra)
    aux = jnp.concatenate([down, extra], 0).astype(BF)
    for k in range(GROUPS):
        outs[k, 4] = aux


def attend_kernel(base, last, flags, packs, gain_q, gain_k, by_frame, within, ups, *refs):
    before = None
    if last:
        before, refs = refs[0], refs[1:]
    wide_out, summed = refs[:2]
    refs = refs[2:]
    if last:
        mean_out, *mix = refs[:4]
        refs = refs[4:]
    q_s, k_s, kt_s, v_s, g_s, sc, dp, pb, db, dk_acc, dv_acc, dq_s, prod_s, sums = refs
    s = lax.axis_index("seq")
    step = pl.program_id(0)
    head = s * LOCAL_HEADS + base + step
    owner = []
    for k in range(GROUPS):
        owner.append(flags[0, k] + (owner[-1] if k else 0))
        at = slice(k * FRAME_TOK, (k + 1) * FRAME_TOK)
        q_s[at, :] = packs[k, 0]
        key = packs[k, 1]
        k_s[at, :] = key
        kt_s[:, at] = key.astype(F32).T.astype(BF)
        v_s[at, :] = packs[k, 2]
        g_s[at, :] = packs[k, 3]
    factor = SCALING * math.log2(math.e)
    lane = lax.broadcasted_iota(jnp.int32, (1, 256), 1)
    for t in range(4):
        b = t % 2
        tile = slice(t * 256, (t + 1) * 256)
        q_t, g_t = q_s[tile, :], g_s[tile, :]
        limit = jnp.where(lane < FRAME_TOK, owner[2 * t], owner[2 * t + 1])
        bias = [jnp.where(owner[j] <= limit, 0.0, HIDDEN) for j in range(GROUPS)]
        sc[b] = nt(k_s[...], q_t)
        dp[b] = nt(v_s[...], g_t)
        top = jnp.full((8, 256), 2.0 * HIDDEN, F32)
        for j in range(GROUPS):
            part = sc[b, j * FRAME_TOK : (j + 1) * FRAME_TOK, :]
            top = jnp.maximum(top, jnp.max(part.reshape(16, 8, 256), axis=0) + bias[j])
        top = jnp.max(top, axis=0, keepdims=True)
        total = jnp.zeros((8, 256), F32)
        cross = jnp.zeros((8, 256), F32)
        for j in range(GROUPS):
            at = slice(j * FRAME_TOK, (j + 1) * FRAME_TOK)
            weight = jnp.exp2((sc[b, at, :] - (top - bias[j])) * factor)
            sc[b, at, :] = weight
            total = total + jnp.sum(weight.reshape(16, 8, 256), axis=0)
            cross = cross + jnp.sum((weight * dp[b, at, :]).reshape(16, 8, 256), axis=0)
        inverse = 1.0 / jnp.sum(total, axis=0, keepdims=True)
        delta = jnp.sum(cross, axis=0, keepdims=True) * inverse
        for j in range(GROUPS):
            at = slice(j * FRAME_TOK, (j + 1) * FRAME_TOK)
            prob = sc[b, at, :] * inverse
            pb[b, at, :] = prob.astype(BF)
            db[b, at, :] = (prob * (dp[b, at, :] - delta)).astype(BF)
        dv, dk = nn(pb[b], g_t), nn(db[b], q_t)
        if t == 0:
            dv_acc[...] = dv
            dk_acc[...] = dk
        else:
            dv_acc[...] += dv
            dk_acc[...] += dk
        dq_s[tile, :] = nn(kt_s[...], db[b]).T
    up_at = pl.ds(pl.multiple_of(head * HEAD_DIM, HEAD_DIM), HEAD_DIM)
    gains = [gain[pl.ds(head, 1), :] for gain in (gain_q, gain_k)]
    for k in range(GROUPS):
        at = slice(k * FRAME_TOK, (k + 1) * FRAME_TOK)
        for n, (acc, rot) in enumerate(((dq_s, q_s), (dk_acc, k_s))):
            grad = (acc[at, :] * SCALING).astype(BF).astype(F32)
            wide = gains[n] * turn(grad, by_frame, within, k, -1)
            wide_out[0, n, at, :] = wide.astype(BF)
            prod_s[n, at, :] = (grad * rot[at, :].astype(F32)).astype(BF)
        wide_out[0, 2, at, :] = dv_acc[at, :].astype(BF)
    ones = jnp.ones((16, HEAD_DIM), BF)
    parts = [nt(ups[n, :, up_at], wide_out[0, n]) for n in range(3)]
    parts += [nt(ones, prod_s[n])[0:8] for n in range(2)]
    full = jnp.concatenate(parts, 0)
    for k in range(GROUPS):
        part = full[:, k * FRAME_TOK : (k + 1) * FRAME_TOK]
        if last:
            sums[k] = part + before[k]
        else:
            summed[k] = part + jnp.where(step > 0, summed[k], 0.0)
    if not last:
        return
    at_row = lax.broadcasted_iota(jnp.int32, (8, FRAME_TOK), 0)
    for n in range(2):
        gathered = jnp.zeros((8, FRAME_TOK), F32)
        for k in range(GROUPS):
            row = sums[jnp.bitwise_xor(s, k), 96 + 8 * n : 104 + 8 * n]
            gathered = jnp.where(at_row == k, row, gathered)
        mean_out[8 * n : 8 * n + 8, :] = gathered
    tail = halves(mean_out[...])
    for b in range(2):
        summed[b] = sums[jnp.bitwise_xor(s, b), 0:96]
        for a in range(1, 4):
            away = jnp.bitwise_xor(s, 2 * a + b)
            mix[a - 1][b * 96 : (b + 1) * 96, :] = sums[away, 0:96].astype(BF)
    for a in range(1, 4):
        mix[a - 1][192:224, :] = tail


def halves(means):
    high = means.astype(BF).astype(F32)
    return jnp.concatenate([high, means - high], 0).astype(BF)


def add_means(got, first, bit):
    tail = got[first : first + 32, :].astype(F32)
    tail = tail[0:16] + tail[16:32]
    moved = [tail[8 * n + (p ^ bit) : 8 * n + (p ^ bit) + 1] for n in range(2) for p in range(8)]
    return jnp.concatenate(moved, 0)


def mix_kernel(keep, means, r1, r2, r3, keep_out, means_out, send):
    total = (means[...] + add_means(r1, 192, 2)) + (add_means(r2, 192, 4) + add_means(r3, 192, 6))
    means_out[...] = total
    for i in range(2):
        at = slice(i * 96, (i + 1) * 96)
        value = keep[i] + r1[at, :].astype(F32)
        value = value + (r2[at, :].astype(F32) + r3[at, :].astype(F32))
        if i == 0:
            keep_out[...] = value
        else:
            send[0:96, :] = value.astype(BF)
    send[96:128, :] = halves(total)


def owner_kernel(kept, means, got, local, tokens, keep, send, means_out, rows_s, mixed_s):
    _, y, x, c = position()
    total = kept[...] + got[0:96, :].astype(F32)
    full = means[...] + add_means(got, 96, 1)
    means_out[...] = full
    for n in range(2):
        at = slice(n * RANK, (n + 1) * RANK)
        rho = local[64 + 8 * n : 65 + 8 * n, :]
        mean = full[8 * n : 8 * n + 1] * (1.0 / CHANNELS)
        rows_s[at, :] = rho * (total[at] - mean * local[at, :])
    rows_s[64:96, :] = total[64:96]
    for k in range(4):
        first = pl.multiple_of(jnp.bitwise_xor(y, k) * 24, 8)
        mixed_s[k * 24 : (k + 1) * 24, :] = rows_s[pl.ds(first, 24), :]
    mixed = mixed_s[...].astype(BF)
    for a in range(2):
        for b in range(4):
            block = jnp.bitwise_xor(c, a) * 4 + jnp.bitwise_xor(x, b)
            at = pl.ds(pl.multiple_of(block * COLS, HEAD_DIM), COLS)
            out = nn(mixed, tokens[:, at])
            for k in range(4):
                part = out[k * 24 : (k + 1) * 24]
                if a == 0:
                    keep[b, k] = part
                else:
                    send[b, k] = part.astype(BF)


def up_kernel(means, firsts, lasts, wide01, wide2, *refs):
    gain_q, gain_k, by_frame, within, keep, send, turned_s, up_s = refs
    wides = [wide01.at[0], wide01.at[1], wide2.at[0]]
    s, _, x, c = position()
    xl = jnp.bitwise_and(x, 1)
    for h in range(LOCAL_HEADS):
        lanes = slice(h * HEAD_DIM, (h + 1) * HEAD_DIM)
        for k in range(GROUPS):
            at = slice(k * FRAME_TOK, (k + 1) * FRAME_TOK)
            for n in range(2):
                rot = (lasts if h == 2 else firsts)[k, 4 * (h % 2) + n].astype(F32)
                turned_s[n, at, lanes] = turn(rot, by_frame, within, k, -1).astype(BF)
    for n in range(3):
        plain_hi, plain_lo, along = [], [], []
        for p in range(GROUPS):
            aux = lasts[p, 4].astype(F32)
            down = aux[n * RANK : (n + 1) * RANK]
            if n == 2:
                plain_hi.append(down.astype(BF))
                continue
            rho = aux[96 + 2 * n : 97 + 2 * n] + aux[97 + 2 * n : 98 + 2 * n]
            mean = means[pl.ds(8 * n + jnp.bitwise_xor(s, p), 1), :]
            scaled = down * rho
            high = scaled.astype(BF)
            plain_hi.append(high)
            plain_lo.append((scaled - high.astype(F32)).astype(BF))
            along.append((scaled * (mean * (1.0 / CHANNELS))).astype(BF))
        high = jnp.concatenate(plain_hi, 1)
        for h in range(LOCAL_HEADS):
            lanes = slice(h * HEAD_DIM, (h + 1) * HEAD_DIM)
            out = nn(high, wides[h][n])
            if n < 2:
                gain = (gain_q, gain_k)[n][pl.ds(s * LOCAL_HEADS + h, 1), :]
                out = out + nn(jnp.concatenate(plain_lo, 1), wides[h][n])
                out = out - nn(jnp.concatenate(along, 1), turned_s[n, :, lanes]) / gain
            up_s[n * RANK : (n + 1) * RANK, lanes] = out
    for a in range(2):
        for b in range(2):
            block = jnp.bitwise_xor(c, a) * 2 + jnp.bitwise_xor(xl, b)
            part = up_s[pl.ds(pl.multiple_of(block * 24, 8), 24), :]
            if a == 0:
                keep[b] = part
            else:
                send[b] = part.astype(BF)


def core_sum_kernel(keep, got, own, *sends):
    for b in range(4):
        value = keep[b] + got[b].astype(F32)
        if b == 0:
            own[...] = value
        else:
            sends[b - 1][...] = value.astype(BF)


def up_core_kernel(keep, got, own, send):
    own[...] = keep[0] + got[0].astype(F32)
    send[...] = (keep[1] + got[1].astype(F32)).astype(BF)


def x_sum_kernel(own, r1, r2, r3, keep, *sends):
    for b in range(4):
        value = (own[b] + r1[b].astype(F32)) + (r2[b].astype(F32) + r3[b].astype(F32))
        if b == 0:
            keep[...] = value
        else:
            sends[b - 1][...] = value.astype(BF)


def y_sum_kernel(own, r1, r2, r3, up_own, up_got, out):
    value = (own[...] + r1[...].astype(F32)) + (r2[...].astype(F32) + r3[...].astype(F32))
    out[:, :COLS] = value.astype(BF)
    out[:, COLS:] = (up_own[...] + up_got[...].astype(F32)).astype(BF)


def z_four_kernel(own, r1, r2, r3, out):
    value = (own[...].astype(F32) + r1[...].astype(F32)) + (r2[...].astype(F32) + r3[...].astype(F32))
    out[...] = value.astype(BF)


def z_sum_kernel(own, got, out):
    out[...] = (own[...].astype(F32) + got[...].astype(F32)).astype(BF)


def stack_kernel(*refs):
    out = refs[-1]
    for n, ref in enumerate(refs[:-1]):
        out[n] = ref[...]


def final_kernel(own, got, down_out, up_out):
    _, y, x, c = position()

    def piece(ca, xa, ya, lanes):
        xr, yr = jnp.bitwise_xor(x, xa), jnp.bitwise_xor(y, ya)
        mine = own[xr, yr, :, lanes].astype(F32)
        other = got[xr, yr, :, lanes].astype(F32)
        return jnp.where(c == ca, mine, other)

    for ca in range(2):
        for xa in range(4):
            block = [piece(ca, xa, ya, slice(0, COLS)) for ya in range(4)]
            first = (ca * 4 + xa) * COLS
            down_out[:, first : first + COLS] = jnp.concatenate(block, 0).astype(BF)
    for ya in range(4):
        for xh in range(2):
            block = [
                piece(ca, xh * 2 + xl, ya, slice(COLS, BOTH)) for ca in range(2) for xl in range(2)
            ]
            first = (ya * 2 + xh) * GCOLS
            up_out[:, first : first + GCOLS] = jnp.concatenate(block, 0).astype(BF)


def shape(dims, dtype=BF):
    return jax.ShapeDtypeStruct(dims, dtype)


def call(kernel, ins, outs, scratch=(), smem=0, mib=16):
    single = not isinstance(outs, (list, tuple))
    return pl.pallas_call(
        kernel,
        out_shape=outs,
        in_specs=[SMEM] * smem + [VMEM] * (len(ins) - smem),
        out_specs=VMEM if single else [VMEM] * len(outs),
        scratch_shapes=list(scratch),
        compiler_params=params(mib),
    )(*ins)


def place(x, y, z, c):
    return (y * 2 + x // 2) * 32 + z * 4 + (x % 2) * 2 + c


def swap(array, dx=0, dy=0, dz=0, dc=0):
    pairs = [
        (place(x, y, z, c), place(x ^ dx, y ^ dy, z ^ dz, c ^ dc))
        for x in range(4)
        for y in range(4)
        for z in range(8)
        for c in range(2)
    ]
    return lax.ppermute(array, ("seq", "dp"), pairs)


def seq_swap(array, k):
    return swap(array, dx=2 * (k & 1), dy=k >> 1)


def whole(array):
    zeros = (0,) * len(array.shape)
    return pl.BlockSpec(array.shape, lambda i: zeros)


def pack(ins, heads, outs, steps):
    count = FRAME_TOK // steps
    specs = [pl.BlockSpec((count, CHANNELS), lambda i: (i, 0))] * 4 + [whole(a) for a in ins[4:]]
    specs[8] = pl.BlockSpec((3, count, HEAD_DIM), lambda i: (0, i, 0))
    slots = outs[0].shape[1]
    out_specs = [pl.BlockSpec((GROUPS, slots, count, HEAD_DIM), lambda i: (0, 0, i, 0))]
    return pl.pallas_call(
        functools.partial(pack_kernel, heads),
        grid=(steps,),
        out_shape=outs,
        in_specs=specs,
        out_specs=out_specs + [whole(a) for a in outs[1:]],
        scratch_shapes=[pltpu.VMEM((FRAME_TOK, FRAME_TOK), F32)],
        compiler_params=params(BIG),
    )(*ins)


def attend(base, heads, ins, before):
    last = before is not None
    seq_len = FRAMES * FRAME_TOK
    rows = (seq_len, HEAD_DIM)
    piece = pl.BlockSpec((GROUPS, 4, FRAME_TOK, HEAD_DIM), lambda i: (0, i, 0, 0))
    specs = [SMEM, piece] + [whole(a) for a in ins[2:]]
    outs = [shape((heads, 3, *rows))]
    out_specs = [pl.BlockSpec((1, 3, *rows), lambda i: (i, 0, 0, 0))]
    if last:
        ins = [*ins, before]
        specs.append(whole(before))
        extra = [shape((2, 96, FRAME_TOK), F32), shape((16, FRAME_TOK), F32)]
        extra += [shape((224, FRAME_TOK))] * 3
        out_specs += [VMEM] * 5
    else:
        extra = [shape((GROUPS, 112, FRAME_TOK), F32)]
        out_specs += [whole(a) for a in extra]
    return pl.pallas_call(
        functools.partial(attend_kernel, base, last),
        grid=(heads,),
        out_shape=outs + extra,
        in_specs=specs,
        out_specs=out_specs,
        scratch_shapes=[
            pltpu.VMEM(rows, BF),
            pltpu.VMEM(rows, BF),
            pltpu.VMEM((HEAD_DIM, seq_len), BF),
            pltpu.VMEM(rows, BF),
            pltpu.VMEM(rows, BF),
            pltpu.VMEM((2, seq_len, 256), F32),
            pltpu.VMEM((2, seq_len, 256), F32),
            pltpu.VMEM((2, seq_len, 256), BF),
            pltpu.VMEM((2, seq_len, 256), BF),
            pltpu.VMEM(rows, F32),
            pltpu.VMEM(rows, F32),
            pltpu.VMEM(rows, F32),
            pltpu.VMEM((2, *rows), BF),
            pltpu.VMEM((GROUPS, 112, FRAME_TOK), F32),
        ],
        compiler_params=params(BIG),
        cost_estimate=pl.CostEstimate(
            flops=10 * heads * seq_len * seq_len * HEAD_DIM,
            bytes_accessed=heads * (4 << 20),
            transcendentals=heads * seq_len * seq_len,
        ),
    )(*ins)


def shards(
    input_tokens,
    query_unnormed,
    key_unnormed,
    value_projected,
    cotangent,
    query_norm_gain,
    key_norm_gain,
    adapter_down_maps,
    adapter_up_maps,
    generated_mask,
    block_begin_flags,
):
    by_frame, within = (jnp.asarray(t) for t in rope_tables())
    gain_q = query_norm_gain.reshape(HEADS, HEAD_DIM)
    gain_k = key_norm_gain.reshape(HEADS, HEAD_DIM)
    norms = [gain_q, gain_k, by_frame, within]
    tokens = input_tokens[0]
    downs = adapter_down_maps.reshape(96, WIDTH)

    raws = [query_unnormed[0], key_unnormed[0], value_projected[0], cotangent[0]]
    first = [*raws, generated_mask[0], *norms]
    (firsts,) = pack(first, (0, 1), [shape((GROUPS, 8, FRAME_TOK, HEAD_DIM))], 4)
    lasts, local = pack(
        first + [adapter_up_maps, downs, tokens],
        (2,),
        [shape((GROUPS, 5, FRAME_TOK, HEAD_DIM)), shape((80, FRAME_TOK), F32)],
        1,
    )
    firsts = lax.all_to_all(firsts, "seq", 0, 0, tiled=True)
    lasts = lax.all_to_all(lasts, "seq", 0, 0, tiled=True)
    shared = [*norms, adapter_up_maps]
    wide01, before = attend(0, 2, [block_begin_flags, firsts, *shared], None)
    wide2, kept, means, *mix = attend(2, 1, [block_begin_flags, lasts, *shared], before)
    mix = [swap(mix[a - 1], dy=a) for a in range(1, 4)]
    kept, means, mix = call(
        mix_kernel,
        [kept, means, *mix],
        [shape((96, FRAME_TOK), F32), shape((16, FRAME_TOK), F32), shape((128, FRAME_TOK))],
    )
    mix = seq_swap(mix, 1)

    keep, send, means = call(
        owner_kernel,
        [kept, means, mix, local, tokens],
        [shape((4, 4, 24, COLS), F32), shape((4, 4, 24, COLS)), shape((16, FRAME_TOK), F32)],
        [pltpu.VMEM((96, FRAME_TOK), F32), pltpu.VMEM((96, FRAME_TOK), F32)],
    )
    up_keep, up_send = call(
        up_kernel,
        [means, firsts, lasts, wide01, wide2, *norms],
        [shape((2, 24, GCOLS), F32), shape((2, 24, GCOLS))],
        [pltpu.VMEM((2, 1024, GCOLS), BF), pltpu.VMEM((96, GCOLS), F32)],
        mib=24,
    )
    got = swap(send, dc=1)
    up_got = swap(up_send, dc=1)
    slab = (4, 24, COLS)
    own, *parts = call(
        core_sum_kernel, [keep, got], [shape(slab, F32)] + [shape(slab)] * 3
    )
    up_own, up_part = call(
        up_core_kernel, [up_keep, up_got], [shape((24, GCOLS), F32), shape((24, GCOLS))]
    )
    parts = [swap(parts[n], dx=n + 1) for n in range(3)]
    up_part = swap(up_part, dx=1)
    own, *parts = call(
        x_sum_kernel, [own, *parts], [shape(slab[1:], F32)] + [shape(slab[1:])] * 3
    )
    parts = [swap(parts[n], dy=n + 1) for n in range(3)]
    part = call(y_sum_kernel, [own, *parts, up_own, up_part], shape((24, BOTH)))
    four = [swap(part, dz=k) for k in range(1, 4)]
    part = call(z_four_kernel, [part, *four], shape((24, BOTH)))
    part = call(z_sum_kernel, [part, swap(part, dz=7)], shape((24, BOTH)))
    over_y = call(
        stack_kernel, [part] + [swap(part, dy=k) for k in range(1, 4)], shape((4, 24, BOTH))
    )
    over_x = call(
        stack_kernel,
        [over_y] + [swap(over_y, dx=k) for k in range(1, 4)],
        shape((4, 4, 24, BOTH)),
    )
    other = swap(over_x, dc=1)
    grad_down, grad_up = call(
        final_kernel,
        [over_x, other],
        [shape((96, WIDTH)), shape((96, CHANNELS))],
    )
    return grad_down.reshape(3, RANK, WIDTH), grad_up.reshape(3, RANK, CHANNELS)


def solution(mesh):
    rows = P("dp", "seq", None)
    placed = (rows,) * 5 + (P(),) * 4 + (rows, P("dp", None))
    return jax.shard_map(shards, mesh=mesh, in_specs=placed, out_specs=(P(), P()), check_vma=False)
```

profile of v0, /device:TPU:1, one launch (start us, length us, event | category | flops | bytes accessed | tf_op | source)
XLA Modules:
  0.0 148.4 jit_solution(8801971500365537941)
XLA Ops:
  0.6 5.2 %shard_map.141 = bf16[8,8,128,128]{3,2,1,0:T(8,128)(2,1)} custom-call(bf16[128,3072]{1,0:T(8,128)(2,1)} %bitcast.23, bf16[128,3072]{1,0:T(8,128)(2,1)} %bitcast.25, bf16[128,3072]{1,0:T(8,128)(2,1)} %bitcast.27, bf16[128,3072]{1,0:T(8,128)(2,1)} %bitcast.29, s32[1,128]{1,0:T(1,128)} %bitcast.32, f32[24,128]{1,0:T(8,128)} %bitcast.13, f32[24,128]{1,0:T(8,128)} %bitcast.18, ...), custom_call_target="tpu_custom_call" | custom-call | tf_op jit(solution)/shard_map/pallas_call | solution.py:454
  5.8 7.5 %all-to-all-start.1 = ((bf16[8,8,128,128]{3,2,1,0:T(8,128)(2,1)}), bf16[8,8,128,128]{3,2,1,0:T(8,128)(2,1)S(1)}, u32[]{:S(2)}, u32[]{:S(2)}) async-start(bf16[8,8,128,128]{3,2,1,0:T(8,128)(2,1)} %shard_map.141), calls=%async_computation.1 | async-start | bytes 4194304 | tf_op jit(solution)/shard_map/all_to_all | solution.py:542
  13.3 5.7 %shard_map.140 = (bf16[8,5,128,128]{3,2,1,0:T(8,128)(2,1)}, f32[80,128]{1,0:T(8,128)}) custom-call(bf16[128,3072]{1,0:T(8,128)(2,1)} %bitcast.24, bf16[128,3072]{1,0:T(8,128)(2,1)} %bitcast.26, bf16[128,3072]{1,0:T(8,128)(2,1)} %bitcast.28, bf16[128,3072]{1,0:T(8,128)(2,1)} %bitcast.30, s32[1,128]{1,0:T(1,128)} %bitcast.33, f32[24,128]{1,0:T(8,128)} %bitcast.14, ...), custom_call_target="tpu_custom_call" | custom-call | tf_op jit(solution)/shard_map/pallas_call | solution.py:454
  19.0 21.9 %all-to-all-done.1.packs.firsts = bf16[8,8,128,128]{3,2,1,0:T(8,128)(2,1)S(1)} async-done(((bf16[8,8,128,128]{3,2,1,0:T(8,128)(2,1)}), bf16[8,8,128,128]{3,2,1,0:T(8,128)(2,1)S(1)}, u32[]{:S(2)}, u32[]{:S(2)}) %all-to-all-start.1) | async-done | bytes 2097184 | tf_op jit(solution)/shard_map/all_to_all | solution.py:542
  40.8 3.8 %all-to-all-start = ((bf16[8,5,128,128]{3,2,1,0:T(8,128)(2,1)}), bf16[8,5,128,128]{3,2,1,0:T(8,128)(2,1)S(1)}, u32[]{:S(2)}, u32[]{:S(2)}) async-start(bf16[8,5,128,128]{3,2,1,0:T(8,128)(2,1)} %get-tuple-element.32), calls=%async_computation | async-start | bytes 2621440 | tf_op jit(solution)/shard_map/all_to_all | solution.py:543
  44.7 12.4 %shard_map.142 = (bf16[2,3,1024,128]{3,2,1,0:T(8,128)(2,1)}, f32[8,112,128]{2,1,0:T(8,128)}) custom-call(s32[1,8]{1,0:T(1,128)} %flags.3, bf16[8,8,128,128]{3,2,1,0:T(8,128)(2,1)} %copy-done, f32[24,128]{1,0:T(8,128)} %bitcast.15, f32[24,128]{1,0:T(8,128)} %bitcast.20, f32[24,128]{1,0:T(8,128)} %constant.4.clone.by_frame.refs_2_, ...), custom_call_target="tpu_custom_call" | custom-call | flops 2684354560 | bytes 8388608 | tf_op jit(solution)/shard_map/pallas_call | solution.py:482
  57.1 5.7 %all-to-all-done.packs.lasts = bf16[8,5,128,128]{3,2,1,0:T(8,128)(2,1)S(1)} async-done(((bf16[8,5,128,128]{3,2,1,0:T(8,128)(2,1)}), bf16[8,5,128,128]{3,2,1,0:T(8,128)(2,1)S(1)}, u32[]{:S(2)}, u32[]{:S(2)}) %all-to-all-start) | async-done | bytes 1310752 | tf_op jit(solution)/shard_map/all_to_all | solution.py:543
  62.8 1.1 copy-done.2
  63.9 7.6 %shard_map.143 = (bf16[1,3,1024,128]{3,2,1,0:T(8,128)(2,1)}, f32[2,96,128]{2,1,0:T(8,128)}, f32[16,128]{1,0:T(8,128)}, bf16[224,128]{1,0:T(8,128)(2,1)}, bf16[22...) custom-call(s32[1,8]{1,0:T(1,128)} %flags.3, bf16[8,5,128,128]{3,2,1,0:T(8,128)(2,1)} %copy-done.2, f32[24,128]{1,0:T(8,128)} %bitcast.16, ...), custom_call_target="tpu_custom_call" | custom-call | flops 1342177280 | bytes 4194304 | tf_op jit(solution)/shard_map/pallas_call | solution.py:482
  71.5 2.1 %collective-permute-start.1 = (bf16[224,128]{1,0:T(8,128)(2,1)}, bf16[224,128]{1,0:T(8,128)(2,1)S(1)}, u32[]{:S(2)}, u32[]{:S(2)}) collective-permute-start(bf16[224,128]{1,0:T(8,128)(2,1)} %get-tuple-element.37), channel_id=1, source_target_pairs={{0,128},{1,129},{4,132},{5,133},{8,136},{9,137},{12,140},{13,141},... | collective-permute-start | bytes 172040 | tf_op jit(solution)/shard_map/ppermute | solution.py:436
  73.6 1.8 %collective-permute-start.2 = (bf16[224,128]{1,0:T(8,128)(2,1)}, bf16[224,128]{1,0:T(8,128)(2,1)S(1)}, u32[]{:S(2)}, u32[]{:S(2)}) collective-permute-start(bf16[224,128]{1,0:T(8,128)(2,1)} %get-tuple-element.38), channel_id=1, source_target_pairs={{0,192},{1,193},{4,196},{5,197},{8,200},{9,201},{12,204},{13,205},... | collective-permute-start | bytes 172040 | tf_op jit(solution)/shard_map/ppermute | solution.py:436
  75.4 1.0 collective-permute-done.1.r2
  76.3 1.7 %collective-permute-done.2.r3 = bf16[224,128]{1,0:T(8,128)(2,1)S(1)} collective-permute-done((bf16[224,128]{1,0:T(8,128)(2,1)}, bf16[224,128]{1,0:T(8,128)(2,1)S(1)}, u32[]{:S(2)}, u32[]{:S(2)}) %collective-permute-start.2) | collective-permute-done | bytes 57376 | tf_op jit(solution)/shard_map/ppermute | solution.py:436
  78.0 0.9 copy-done.11
  78.9 0.7 copy-done.13
  79.7 3.3 %collective-permute-start.3 = (bf16[128,128]{1,0:T(8,128)(2,1)S(1)}, bf16[128,128]{1,0:T(8,128)(2,1)S(1)}, u32[]{:S(2)}, u32[]{:S(2)}) collective-permute-start(bf16[128,128]{1,0:T(8,128)(2,1)S(1)} %get-tuple-element.41), channel_id=1, source_target_pairs={{0,32},{1,33},{4,36},{5,37},{8,40},{9,41},{12,44},{13,45},{16,48},... | collective-permute-start | bytes 98312 | tf_op jit(solution)/shard_map/ppermute | solution.py:436
  83.0 1.3 collective-permute-done.3.got
  84.3 0.4 shard_map.145
  84.8 5.2 %collective-permute-start.4 = (bf16[4,4,24,640]{3,2,1,0:T(8,128)(2,1)S(1)}, bf16[4,4,24,640]{3,2,1,0:T(8,128)(2,1)S(1)}, u32[]{:S(2)}, u32[]{:S(2)}) collective-permute-start(bf16[4,4,24,640]{3,2,1,0:T(8,128)(2,1)S(1)} %get-tuple-element.44), channel_id=1, source_target_pairs={{0,1},{1,0},{4,5},{5,4},{8,9},{9,8},{12,13},{13,12},{16,17},{17,16... | collective-permute-start | bytes 1474568 | tf_op jit(solution)/shard_map/ppermute | solution.py:436
  90.0 1.5 %collective-permute-done.4.got = bf16[4,4,24,640]{3,2,1,0:T(8,128)(2,1)S(1)} collective-permute-done((bf16[4,4,24,640]{3,2,1,0:T(8,128)(2,1)S(1)}, bf16[4,4,24,640]{3,2,1,0:T(8,128)(2,1)S(1)}, u32[]{:S(2)}, u32[]{:S(2)}) %collective-permute-start.4) | collective-permute-done | bytes 491552 | tf_op jit(solution)/shard_map/ppermute | solution.py:436
  91.5 0.4 collective-permute-start.5
  91.9 1.5 %collective-permute-start.6 = (bf16[4,24,640]{2,1,0:T(8,128)(2,1)S(1)}, bf16[4,24,640]{2,1,0:T(8,128)(2,1)S(1)}, u32[]{:S(2)}, u32[]{:S(2)}) collective-permute-start(bf16[4,24,640]{2,1,0:T(8,128)(2,1)S(1)} %get-tuple-element.47), channel_id=1, source_target_pairs={{0,32},{1,33},{4,36},{5,37},{8,40},{9,41},{12,44},{13,45},{16,48},... | collective-permute-start | bytes 368648 | tf_op jit(solution)/shard_map/ppermute | solution.py:436
  93.4 2.1 %collective-permute-start.7 = (bf16[4,24,640]{2,1,0:T(8,128)(2,1)S(1)}, bf16[4,24,640]{2,1,0:T(8,128)(2,1)S(1)}, u32[]{:S(2)}, u32[]{:S(2)}) collective-permute-start(bf16[4,24,640]{2,1,0:T(8,128)(2,1)S(1)} %get-tuple-element.48), channel_id=1, source_target_pairs={{0,34},{1,35},{4,38},{5,39},{8,42},{9,43},{12,46},{13,47},{16,50},... | collective-permute-start | bytes 368648 | tf_op jit(solution)/shard_map/ppermute | solution.py:436
  95.5 1.3 copy-done.3
  96.8 1.9 %shard_map.148 = (f32[2,24,384]{2,1,0:T(8,128)S(1)}, bf16[2,24,384]{2,1,0:T(8,128)(2,1)S(1)}) custom-call(f32[16,128]{1,0:T(8,128)S(1)} %get-tuple-element.53.means, bf16[8,8,128,128]{3,2,1,0:T(8,128)(2,1)S(1)} %copy-done.1, bf16[8,5,128,128]{3,2,1,0:T(8,128)(2,1)S(1)} %copy-done.3, bf16[2,3,1024,128]{3,2,1,0:T(8,128)(2,1)S(1)} %copy-done.6, ...), custom_call_target="tpu_custom_call" | custom-call | tf_op jit(solution)/shard_map/pallas_call | solution.py:414
  98.8 1.3 collective-permute-start.11
  100.1 1.6 %collective-permute-done.7.r3 = bf16[4,24,640]{2,1,0:T(8,128)(2,1)S(1)} collective-permute-done((bf16[4,24,640]{2,1,0:T(8,128)(2,1)S(1)}, bf16[4,24,640]{2,1,0:T(8,128)(2,1)S(1)}, u32[]{:S(2)}, u32[]{:S(2)}) %collective-permute-start.7) | collective-permute-done | bytes 122912 | tf_op jit(solution)/shard_map/ppermute | solution.py:436
  101.8 3.0 %collective-permute-start.9 = (bf16[24,640]{1,0:T(8,128)(2,1)S(1)}, bf16[24,640]{1,0:T(8,128)(2,1)S(1)}, u32[]{:S(2)}, u32[]{:S(2)}) collective-permute-start(bf16[24,640]{1,0:T(8,128)(2,1)S(1)} %get-tuple-element.51), channel_id=1, source_target_pairs={{0,128},{1,129},{4,132},{5,133},{8,136},{9,137},{12,140},{13,141},... | collective-permute-start | bytes 92168 | tf_op jit(solution)/shard_map/ppermute | solution.py:436
  104.8 0.9 collective-permute-start.10
  105.8 2.6 %collective-permute-done.12.up_got = bf16[24,384]{1,0:T(8,128)(2,1)S(1)} collective-permute-done((bf16[24,384]{1,0:T(8,128)(2,1)S(1)}, bf16[24,384]{1,0:T(8,128)(2,1)S(1)}, u32[]{:S(2)}, u32[]{:S(2)}) %collective-permute-start.12) | collective-permute-done | bytes 18464 | tf_op jit(solution)/shard_map/ppermute | solution.py:436
  108.4 0.3 collective-permute-done.10.r3
  108.8 4.4 %collective-permute-start.15 = (bf16[24,1024]{1,0:T(8,128)(2,1)S(1)}, bf16[24,1024]{1,0:T(8,128)(2,1)S(1)}, u32[]{:S(2)}, u32[]{:S(2)}) collective-permute-start(bf16[24,1024]{1,0:T(8,128)(2,1)S(1)} %shard_map.150.own), channel_id=1, source_target_pairs={{0,12},{1,13},{4,8},{5,9},{8,4},{9,5},{12,0},{13,1},{16,28},{17,29... | collective-permute-start | bytes 147464 | tf_op jit(solution)/shard_map/ppermute | solution.py:436
  113.2 0.4 collective-permute-start.13
  113.6 1.1 collective-permute-done.15.r3
  114.7 2.7 %collective-permute-done.14.r2 = bf16[24,1024]{1,0:T(8,128)(2,1)S(1)} collective-permute-done((bf16[24,1024]{1,0:T(8,128)(2,1)S(1)}, bf16[24,1024]{1,0:T(8,128)(2,1)S(1)}, u32[]{:S(2)}, u32[]{:S(2)}) %collective-permute-start.14) | collective-permute-done | bytes 49184 | tf_op jit(solution)/shard_map/ppermute | solution.py:436
  117.4 3.0 %collective-permute-start.16 = (bf16[24,1024]{1,0:T(8,128)(2,1)S(1)}, bf16[24,1024]{1,0:T(8,128)(2,1)S(1)}, u32[]{:S(2)}, u32[]{:S(2)}) collective-permute-start(bf16[24,1024]{1,0:T(8,128)(2,1)S(1)} %shard_map.151.own), channel_id=1, source_target_pairs={{0,28},{1,29},{4,24},{5,25},{8,20},{9,21},{12,16},{13,17},{16,12},... | collective-permute-start | bytes 147464 | tf_op jit(solution)/shard_map/ppermute | solution.py:436
  120.4 1.5 collective-permute-done.16.got
  121.9 1.9 %collective-permute-start.19 = (bf16[24,1024]{1,0:T(8,128)(2,1)S(1)}, bf16[24,1024]{1,0:T(8,128)(2,1)S(1)}, u32[]{:S(2)}, u32[]{:S(2)}) collective-permute-start(bf16[24,1024]{1,0:T(8,128)(2,1)S(1)} %shard_map.152.refs_0_), channel_id=1, source_target_pairs={{0,192},{1,193},{4,196},{5,197},{8,200},{9,201},{12,204},{13,205},... | collective-permute-start | bytes 147464 | tf_op jit(solution)/shard_map/ppermute | solution.py:436
  123.7 1.7 %collective-permute-start.17 = (bf16[24,1024]{1,0:T(8,128)(2,1)S(1)}, bf16[24,1024]{1,0:T(8,128)(2,1)S(1)}, u32[]{:S(2)}, u32[]{:S(2)}) collective-permute-start(bf16[24,1024]{1,0:T(8,128)(2,1)S(1)} %shard_map.152.refs_0_), channel_id=1, source_target_pairs={{0,64},{1,65},{4,68},{5,69},{8,72},{9,73},{12,76},{13,77},{16,80},... | collective-permute-start | bytes 147464 | tf_op jit(solution)/shard_map/ppermute | solution.py:436
  125.4 1.2 collective-permute-done.19.refs_3_
  126.6 1.6 %collective-permute-done.18.refs_2_ = bf16[24,1024]{1,0:T(8,128)(2,1)S(1)} collective-permute-done((bf16[24,1024]{1,0:T(8,128)(2,1)S(1)}, bf16[24,1024]{1,0:T(8,128)(2,1)S(1)}, u32[]{:S(2)}, u32[]{:S(2)}) %collective-permute-start.18) | collective-permute-done | bytes 49184 | tf_op jit(solution)/shard_map/ppermute | solution.py:436
  128.2 2.4 %collective-permute-start.22 = (bf16[4,24,1024]{2,1,0:T(8,128)(2,1)S(1)}, bf16[4,24,1024]{2,1,0:T(8,128)(2,1)S(1)}, u32[]{:S(2)}, u32[]{:S(2)}) collective-permute-start(bf16[4,24,1024]{2,1,0:T(8,128)(2,1)S(1)} %shard_map.153.refs_0_), channel_id=1, source_target_pairs={{0,34},{1,35},{4,38},{5,39},{8,42},{9,43},{12,46},{13,47},{16,50},... | collective-permute-start | bytes 589832 | tf_op jit(solution)/shard_map/ppermute | solution.py:436
  130.8 0.7 collective-permute-start.20
  131.6 3.8 %collective-permute-done.22.refs_3_ = bf16[4,24,1024]{2,1,0:T(8,128)(2,1)S(1)} collective-permute-done((bf16[4,24,1024]{2,1,0:T(8,128)(2,1)S(1)}, bf16[4,24,1024]{2,1,0:T(8,128)(2,1)S(1)}, u32[]{:S(2)}, u32[]{:S(2)}) %collective-permute-start.22) | collective-permute-done | bytes 196640 | tf_op jit(solution)/shard_map/ppermute | solution.py:436
  135.4 1.3 collective-permute-done.21.refs_2_
  136.8 8.3 %collective-permute-start.23 = (bf16[4,4,24,1024]{3,2,1,0:T(8,128)(2,1)S(1)}, bf16[4,4,24,1024]{3,2,1,0:T(8,128)(2,1)S(1)}, u32[]{:S(2)}, u32[]{:S(2)}) collective-permute-start(bf16[4,4,24,1024]{3,2,1,0:T(8,128)(2,1)S(1)} %shard_map.154.own), channel_id=1, source_target_pairs={{0,1},{1,0},{4,5},{5,4},{8,9},{9,8},{12,13},{13,12},{16,17},{17,16... | collective-permute-start | bytes 2359304 | tf_op jit(solution)/shard_map/ppermute | solution.py:436
  145.1 1.9 %collective-permute-done.23.got = bf16[4,4,24,1024]{3,2,1,0:T(8,128)(2,1)S(1)} collective-permute-done((bf16[4,4,24,1024]{3,2,1,0:T(8,128)(2,1)S(1)}, bf16[4,4,24,1024]{3,2,1,0:T(8,128)(2,1)S(1)}, u32[]{:S(2)}, u32[]{:S(2)}) %collective-permute-start.23) | collective-permute-done | bytes 786464 | tf_op jit(solution)/shard_map/ppermute | solution.py:436
  147.0 1.4 shard_map.155
  (48 shorter events, 0.8 us)
Async XLA Ops:
  5.8 35.0 %all-to-all-start.1 = ((bf16[8,8,128,128]{3,2,1,0:T(8,128)(2,1)}), bf16[8,8,128,128]{3,2,1,0:T(8,128)(2,1)S(1)}, u32[]{:S(2)}, u32[]{:S(2)}) async-start(bf16[8,8,128,128]{3,2,1,0:T(8,128)(2,1)} %shard_map.141), calls=%async_computation.1 | async-start | bytes 4194304 | tf_op jit(solution)/shard_map/all_to_all | solution.py:542
  40.8 3.8 %copy-start = (bf16[8,8,128,128]{3,2,1,0:T(8,128)(2,1)}, bf16[8,8,128,128]{3,2,1,0:T(8,128)(2,1)S(1)}, u32[]{:S(2)}) copy-start(bf16[8,8,128,128]{3,2,1,0:T(8,128)(2,1)S(1)} %all-to-all-done.1.packs.firsts) | copy-start | bytes 6291460
  40.8 22.0 %all-to-all-start = ((bf16[8,5,128,128]{3,2,1,0:T(8,128)(2,1)}), bf16[8,5,128,128]{3,2,1,0:T(8,128)(2,1)S(1)}, u32[]{:S(2)}, u32[]{:S(2)}) async-start(bf16[8,5,128,128]{3,2,1,0:T(8,128)(2,1)} %get-tuple-element.32), calls=%async_computation | async-start | bytes 2621440 | tf_op jit(solution)/shard_map/all_to_all | solution.py:543
  62.8 1.1 copy-start.2
  63.9 20.4 %copy-start.4 = (bf16[1,128,5120]{2,1,0:T(8,128)(2,1)S(1)}, bf16[1,128,5120]{2,1,0:T(8,128)(2,1)}, u32[]{:S(2)}) copy-start(bf16[1,128,5120]{2,1,0:T(8,128)(2,1)} %param.13) | copy-start | bytes 3932164
  63.9 20.4 %copy-start.12 = (f32[80,128]{1,0:T(8,128)S(1)}, f32[80,128]{1,0:T(8,128)}, u32[]{:S(2)}) copy-start(f32[80,128]{1,0:T(8,128)} %get-tuple-element.42.local) | copy-start | bytes 122884
  63.9 31.5 %copy-start.6 = (bf16[2,3,1024,128]{3,2,1,0:T(8,128)(2,1)S(1)}, bf16[2,3,1024,128]{3,2,1,0:T(8,128)(2,1)}, u32[]{:S(2)}) copy-start(bf16[2,3,1024,128]{3,2,1,0:T(8,128)(2,1)} %get-tuple-element.54.wide01) | copy-start | bytes 4718596
  71.5 3.9 %collective-permute-start = (bf16[224,128]{1,0:T(8,128)(2,1)}, bf16[224,128]{1,0:T(8,128)(2,1)S(1)}, u32[]{:S(2)}, u32[]{:S(2)}) collective-permute-start(bf16[224,128]{1,0:T(8,128)(2,1)} %get-tuple-element.36), channel_id=1, source_target_pairs={{0,64},{1,65},{4,68},{5,69},{8,72},{9,73},{12,76},{13,77},{16,80},... | collective-permute-start | bytes 172040 | tf_op jit(solution)/shard_map/ppermute | solution.py:436
  71.5 4.8 %collective-permute-start.1 = (bf16[224,128]{1,0:T(8,128)(2,1)}, bf16[224,128]{1,0:T(8,128)(2,1)S(1)}, u32[]{:S(2)}, u32[]{:S(2)}) collective-permute-start(bf16[224,128]{1,0:T(8,128)(2,1)} %get-tuple-element.37), channel_id=1, source_target_pairs={{0,128},{1,129},{4,132},{5,133},{8,136},{9,137},{12,140},{13,141},... | collective-permute-start | bytes 172040 | tf_op jit(solution)/shard_map/ppermute | solution.py:436
  73.6 4.4 %collective-permute-start.2 = (bf16[224,128]{1,0:T(8,128)(2,1)}, bf16[224,128]{1,0:T(8,128)(2,1)S(1)}, u32[]{:S(2)}, u32[]{:S(2)}) collective-permute-start(bf16[224,128]{1,0:T(8,128)(2,1)} %get-tuple-element.38), channel_id=1, source_target_pairs={{0,192},{1,193},{4,196},{5,197},{8,200},{9,201},{12,204},{13,205},... | collective-permute-start | bytes 172040 | tf_op jit(solution)/shard_map/ppermute | solution.py:436
  78.0 0.9 copy-start.11
  78.9 0.7 copy-start.13
  79.6 15.9 %copy-start.1 = (bf16[8,8,128,128]{3,2,1,0:T(8,128)(2,1)S(1)}, bf16[8,8,128,128]{3,2,1,0:T(8,128)(2,1)}, u32[]{:S(2)}) copy-start(bf16[8,8,128,128]{3,2,1,0:T(8,128)(2,1)} %copy-done) | copy-start | bytes 6291460
  79.6 15.9 %copy-start.5 = (f32[3,128,128]{2,1,0:T(8,128)S(1)}, f32[3,128,128]{2,1,0:T(8,128)}, u32[]{:S(2)}) copy-start(f32[3,128,128]{2,1,0:T(8,128)} %constant.5.clone.within.refs_3_) | copy-start | bytes 589828
  79.6 15.9 %copy-start.7 = (bf16[1,3,1024,128]{3,2,1,0:T(8,128)(2,1)S(1)}, bf16[1,3,1024,128]{3,2,1,0:T(8,128)(2,1)}, u32[]{:S(2)}) copy-start(bf16[1,3,1024,128]{3,2,1,0:T(8,128)(2,1)} %get-tuple-element.55.wide2) | copy-start | bytes 2359300
  79.6 15.9 %copy-start.8 = (f32[3072]{0:T(1024)S(1)}, f32[3072]{0:T(1024)}, u32[]{:S(2)}) copy-start(f32[3072]{0:T(1024)} %param.18) | copy-start | bytes 36868
  79.6 15.9 %copy-start.9 = (f32[3072]{0:T(1024)S(1)}, f32[3072]{0:T(1024)}, u32[]{:S(2)}) copy-start(f32[3072]{0:T(1024)} %param.19) | copy-start | bytes 36868
  79.6 15.9 %copy-start.10 = (f32[24,128]{1,0:T(8,128)S(1)}, f32[24,128]{1,0:T(8,128)}, u32[]{:S(2)}) copy-start(f32[24,128]{1,0:T(8,128)} %constant.4.clone.by_frame.refs_2_) | copy-start | bytes 36868
  79.7 4.6 %collective-permute-start.3 = (bf16[128,128]{1,0:T(8,128)(2,1)S(1)}, bf16[128,128]{1,0:T(8,128)(2,1)S(1)}, u32[]{:S(2)}, u32[]{:S(2)}) collective-permute-start(bf16[128,128]{1,0:T(8,128)(2,1)S(1)} %get-tuple-element.41), channel_id=1, source_target_pairs={{0,32},{1,33},{4,36},{5,37},{8,40},{9,41},{12,44},{13,45},{16,48},... | collective-permute-start | bytes 98312 | tf_op jit(solution)/shard_map/ppermute | solution.py:436
  84.8 6.7 %collective-permute-start.4 = (bf16[4,4,24,640]{3,2,1,0:T(8,128)(2,1)S(1)}, bf16[4,4,24,640]{3,2,1,0:T(8,128)(2,1)S(1)}, u32[]{:S(2)}, u32[]{:S(2)}) collective-permute-start(bf16[4,4,24,640]{3,2,1,0:T(8,128)(2,1)S(1)} %get-tuple-element.44), channel_id=1, source_target_pairs={{0,1},{1,0},{4,5},{5,4},{8,9},{9,8},{12,13},{13,12},{16,17},{17,16... | collective-permute-start | bytes 1474568 | tf_op jit(solution)/shard_map/ppermute | solution.py:436
  91.5 8.6 %collective-permute-start.5 = (bf16[4,24,640]{2,1,0:T(8,128)(2,1)S(1)}, bf16[4,24,640]{2,1,0:T(8,128)(2,1)S(1)}, u32[]{:S(2)}, u32[]{:S(2)}) collective-permute-start(bf16[4,24,640]{2,1,0:T(8,128)(2,1)S(1)} %get-tuple-element.46), channel_id=1, source_target_pairs={{0,2},{1,3},{4,6},{5,7},{8,10},{9,11},{12,14},{13,15},{16,18},{17,... | collective-permute-start | bytes 368648 | tf_op jit(solution)/shard_map/ppermute | solution.py:436
  91.9 8.2 %collective-permute-start.6 = (bf16[4,24,640]{2,1,0:T(8,128)(2,1)S(1)}, bf16[4,24,640]{2,1,0:T(8,128)(2,1)S(1)}, u32[]{:S(2)}, u32[]{:S(2)}) collective-permute-start(bf16[4,24,640]{2,1,0:T(8,128)(2,1)S(1)} %get-tuple-element.47), channel_id=1, source_target_pairs={{0,32},{1,33},{4,36},{5,37},{8,40},{9,41},{12,44},{13,45},{16,48},... | collective-permute-start | bytes 368648 | tf_op jit(solution)/shard_map/ppermute | solution.py:436
  93.4 8.2 %collective-permute-start.7 = (bf16[4,24,640]{2,1,0:T(8,128)(2,1)S(1)}, bf16[4,24,640]{2,1,0:T(8,128)(2,1)S(1)}, u32[]{:S(2)}, u32[]{:S(2)}) collective-permute-start(bf16[4,24,640]{2,1,0:T(8,128)(2,1)S(1)} %get-tuple-element.48), channel_id=1, source_target_pairs={{0,34},{1,35},{4,38},{5,39},{8,42},{9,43},{12,46},{13,47},{16,50},... | collective-permute-start | bytes 368648 | tf_op jit(solution)/shard_map/ppermute | solution.py:436
  95.5 1.3 copy-start.3
  98.8 6.9 %collective-permute-start.11 = (bf16[2,24,384]{2,1,0:T(8,128)(2,1)S(1)}, bf16[2,24,384]{2,1,0:T(8,128)(2,1)S(1)}, u32[]{:S(2)}, u32[]{:S(2)}) collective-permute-start(bf16[2,24,384]{2,1,0:T(8,128)(2,1)S(1)} %get-tuple-element.57), channel_id=1, source_target_pairs={{0,1},{1,0},{4,5},{5,4},{8,9},{9,8},{12,13},{13,12},{16,17},{17,16... | collective-permute-start | bytes 110600 | tf_op jit(solution)/shard_map/ppermute | solution.py:436
  101.7 6.7 %collective-permute-start.8 = (bf16[24,640]{1,0:T(8,128)(2,1)S(1)}, bf16[24,640]{1,0:T(8,128)(2,1)S(1)}, u32[]{:S(2)}, u32[]{:S(2)}) collective-permute-start(bf16[24,640]{1,0:T(8,128)(2,1)S(1)} %get-tuple-element.50), channel_id=1, source_target_pairs={{0,64},{1,65},{4,68},{5,69},{8,72},{9,73},{12,76},{13,77},{16,80},... | collective-permute-start | bytes 92168 | tf_op jit(solution)/shard_map/ppermute | solution.py:436
  101.8 6.6 %collective-permute-start.9 = (bf16[24,640]{1,0:T(8,128)(2,1)S(1)}, bf16[24,640]{1,0:T(8,128)(2,1)S(1)}, u32[]{:S(2)}, u32[]{:S(2)}) collective-permute-start(bf16[24,640]{1,0:T(8,128)(2,1)S(1)} %get-tuple-element.51), channel_id=1, source_target_pairs={{0,128},{1,129},{4,132},{5,133},{8,136},{9,137},{12,140},{13,141},... | collective-permute-start | bytes 92168 | tf_op jit(solution)/shard_map/ppermute | solution.py:436
  104.8 4.0 %collective-permute-start.10 = (bf16[24,640]{1,0:T(8,128)(2,1)S(1)}, bf16[24,640]{1,0:T(8,128)(2,1)S(1)}, u32[]{:S(2)}, u32[]{:S(2)}) collective-permute-start(bf16[24,640]{1,0:T(8,128)(2,1)S(1)} %get-tuple-element.52), channel_id=1, source_target_pairs={{0,192},{1,193},{4,196},{5,197},{8,200},{9,201},{12,204},{13,205},... | collective-permute-start | bytes 92168 | tf_op jit(solution)/shard_map/ppermute | solution.py:436
  105.7 2.7 %collective-permute-start.12 = (bf16[24,384]{1,0:T(8,128)(2,1)S(1)}, bf16[24,384]{1,0:T(8,128)(2,1)S(1)}, u32[]{:S(2)}, u32[]{:S(2)}) collective-permute-start(bf16[24,384]{1,0:T(8,128)(2,1)S(1)} %get-tuple-element.59), channel_id=1, source_target_pairs={{0,2},{1,3},{4,6},{5,7},{8,10},{9,11},{12,14},{13,15},{16,18},{17,... | collective-permute-start | bytes 55304 | tf_op jit(solution)/shard_map/ppermute | solution.py:436
  108.8 5.9 %collective-permute-start.15 = (bf16[24,1024]{1,0:T(8,128)(2,1)S(1)}, bf16[24,1024]{1,0:T(8,128)(2,1)S(1)}, u32[]{:S(2)}, u32[]{:S(2)}) collective-permute-start(bf16[24,1024]{1,0:T(8,128)(2,1)S(1)} %shard_map.150.own), channel_id=1, source_target_pairs={{0,12},{1,13},{4,8},{5,9},{8,4},{9,5},{12,0},{13,1},{16,28},{17,29... | collective-permute-start | bytes 147464 | tf_op jit(solution)/shard_map/ppermute | solution.py:436
  113.2 4.1 %collective-permute-start.14 = (bf16[24,1024]{1,0:T(8,128)(2,1)S(1)}, bf16[24,1024]{1,0:T(8,128)(2,1)S(1)}, u32[]{:S(2)}, u32[]{:S(2)}) collective-permute-start(bf16[24,1024]{1,0:T(8,128)(2,1)S(1)} %shard_map.150.own), channel_id=1, source_target_pairs={{0,8},{1,9},{4,12},{5,13},{8,0},{9,1},{12,4},{13,5},{16,24},{17,25... | collective-permute-start | bytes 147464 | tf_op jit(solution)/shard_map/ppermute | solution.py:436
  113.2 4.1 %collective-permute-start.13 = (bf16[24,1024]{1,0:T(8,128)(2,1)S(1)}, bf16[24,1024]{1,0:T(8,128)(2,1)S(1)}, u32[]{:S(2)}, u32[]{:S(2)}) collective-permute-start(bf16[24,1024]{1,0:T(8,128)(2,1)S(1)} %shard_map.150.own), channel_id=1, source_target_pairs={{0,4},{1,5},{4,0},{5,1},{8,12},{9,13},{12,8},{13,9},{16,20},{17,21... | collective-permute-start | bytes 147464 | tf_op jit(solution)/shard_map/ppermute | solution.py:436
  117.4 4.5 %collective-permute-start.16 = (bf16[24,1024]{1,0:T(8,128)(2,1)S(1)}, bf16[24,1024]{1,0:T(8,128)(2,1)S(1)}, u32[]{:S(2)}, u32[]{:S(2)}) collective-permute-start(bf16[24,1024]{1,0:T(8,128)(2,1)S(1)} %shard_map.151.own), channel_id=1, source_target_pairs={{0,28},{1,29},{4,24},{5,25},{8,20},{9,21},{12,16},{13,17},{16,12},... | collective-permute-start | bytes 147464 | tf_op jit(solution)/shard_map/ppermute | solution.py:436
  121.9 4.8 %collective-permute-start.19 = (bf16[24,1024]{1,0:T(8,128)(2,1)S(1)}, bf16[24,1024]{1,0:T(8,128)(2,1)S(1)}, u32[]{:S(2)}, u32[]{:S(2)}) collective-permute-start(bf16[24,1024]{1,0:T(8,128)(2,1)S(1)} %shard_map.152.refs_0_), channel_id=1, source_target_pairs={{0,192},{1,193},{4,196},{5,197},{8,200},{9,201},{12,204},{13,205},... | collective-permute-start | bytes 147464 | tf_op jit(solution)/shard_map/ppermute | solution.py:436
  123.7 4.4 %collective-permute-start.18 = (bf16[24,1024]{1,0:T(8,128)(2,1)S(1)}, bf16[24,1024]{1,0:T(8,128)(2,1)S(1)}, u32[]{:S(2)}, u32[]{:S(2)}) collective-permute-start(bf16[24,1024]{1,0:T(8,128)(2,1)S(1)} %shard_map.152.refs_0_), channel_id=1, source_target_pairs={{0,128},{1,129},{4,132},{5,133},{8,136},{9,137},{12,140},{13,141},... | collective-permute-start | bytes 147464 | tf_op jit(solution)/shard_map/ppermute | solution.py:436
  123.7 4.4 %collective-permute-start.17 = (bf16[24,1024]{1,0:T(8,128)(2,1)S(1)}, bf16[24,1024]{1,0:T(8,128)(2,1)S(1)}, u32[]{:S(2)}, u32[]{:S(2)}) collective-permute-start(bf16[24,1024]{1,0:T(8,128)(2,1)S(1)} %shard_map.152.refs_0_), channel_id=1, source_target_pairs={{0,64},{1,65},{4,68},{5,69},{8,72},{9,73},{12,76},{13,77},{16,80},... | collective-permute-start | bytes 147464 | tf_op jit(solution)/shard_map/ppermute | solution.py:436
  128.2 7.2 %collective-permute-start.22 = (bf16[4,24,1024]{2,1,0:T(8,128)(2,1)S(1)}, bf16[4,24,1024]{2,1,0:T(8,128)(2,1)S(1)}, u32[]{:S(2)}, u32[]{:S(2)}) collective-permute-start(bf16[4,24,1024]{2,1,0:T(8,128)(2,1)S(1)} %shard_map.153.refs_0_), channel_id=1, source_target_pairs={{0,34},{1,35},{4,38},{5,39},{8,42},{9,43},{12,46},{13,47},{16,50},... | collective-permute-start | bytes 589832 | tf_op jit(solution)/shard_map/ppermute | solution.py:436
  130.7 6.0 %collective-permute-start.21 = (bf16[4,24,1024]{2,1,0:T(8,128)(2,1)S(1)}, bf16[4,24,1024]{2,1,0:T(8,128)(2,1)S(1)}, u32[]{:S(2)}, u32[]{:S(2)}) collective-permute-start(bf16[4,24,1024]{2,1,0:T(8,128)(2,1)S(1)} %shard_map.153.refs_0_), channel_id=1, source_target_pairs={{0,32},{1,33},{4,36},{5,37},{8,40},{9,41},{12,44},{13,45},{16,48},... | collective-permute-start | bytes 589832 | tf_op jit(solution)/shard_map/ppermute | solution.py:436
  130.8 6.0 %collective-permute-start.20 = (bf16[4,24,1024]{2,1,0:T(8,128)(2,1)S(1)}, bf16[4,24,1024]{2,1,0:T(8,128)(2,1)S(1)}, u32[]{:S(2)}, u32[]{:S(2)}) collective-permute-start(bf16[4,24,1024]{2,1,0:T(8,128)(2,1)S(1)} %shard_map.153.refs_0_), channel_id=1, source_target_pairs={{0,2},{1,3},{4,6},{5,7},{8,10},{9,11},{12,14},{13,15},{16,18},{17,... | collective-permute-start | bytes 589832 | tf_op jit(solution)/shard_map/ppermute | solution.py:436
  136.8 10.2 %collective-permute-start.23 = (bf16[4,4,24,1024]{3,2,1,0:T(8,128)(2,1)S(1)}, bf16[4,4,24,1024]{3,2,1,0:T(8,128)(2,1)S(1)}, u32[]{:S(2)}, u32[]{:S(2)}) collective-permute-start(bf16[4,4,24,1024]{3,2,1,0:T(8,128)(2,1)S(1)} %shard_map.154.own), channel_id=1, source_target_pairs={{0,1},{1,0},{4,5},{5,4},{8,9},{9,8},{12,13},{13,12},{16,17},{17,16... | collective-permute-start | bytes 2359304 | tf_op jit(solution)/shard_map/ppermute | solution.py:436
where the time goes:
time: 149 us; the launch traced here: 148 us
  starting transfers between devices  55.9 us (38%)
  waiting for transfers between devices  52.7 us (35%)
  Pallas kernels  35 us (23%)
  local copies, waits for them, and re-layouts  4.05 us (3%)
    ppermute x24, starting transfers between devices, swap(): return lax.ppermute(array, ('seq', 'dp'), pairs)  44.6 us
    ppermute x24, waiting for transfers between devices, swap(): return lax.ppermute(array, ('seq', 'dp'), pairs)  25.1 us
    all_to_all x1, waiting for transfers between devices, shards(): firsts = lax.all_to_all(firsts, 'seq', 0, 0, tiled=True)  21.9 us
    pallas_call x2, Pallas kernels, attend(): pl.pallas_call(functools.partial(attend_kernel, base, last), grid=(heads,...  20 us
    pallas_call x2, Pallas kernels, pack(): pl.pallas_call(functools.partial(pack_kernel, heads), grid=(steps,), out_...  10.9 us
    all_to_all x1, starting transfers between devices, shards(): firsts = lax.all_to_all(firsts, 'seq', 0, 0, tiled=True)  7.48 us
    all_to_all x1, waiting for transfers between devices, shards(): lasts = lax.all_to_all(lasts, 'seq', 0, 0, tiled=True)  5.72 us
    pallas_call x12, Pallas kernels, call(): pl.pallas_call(kernel, out_shape=outs, in_specs=[SMEM] * smem + [VMEM] *...  4.12 us
  transfers between devices with their start and end apart: 26, of which 18 were waited for; matrix products, arithmetic and copies ran while one was open for 0% of the time, Pallas kernels for 14%

commit v1 on v0

--- a/solution.py
+++ b/solution.py
@@ -25,6 +25,7 @@
 F32 = jnp.float32
 HIDDEN = -1e30
 BIG = 58
+HELD = FRAMES * 112
 COLS = WIDTH // 8
 GCOLS = CHANNELS // 8
 BOTH = COLS + GCOLS
@@ -63,10 +64,12 @@
     return by_frame.reshape(3 * FRAMES, HEAD_DIM).astype(np.float32), within.astype(np.float32)
 
 
-def turn(z, by_frame, within, frame, sign):
-    cosine, left, right = (
-        within[n] + by_frame[pl.ds(3 * frame + n, 1), :] for n in range(3)
-    )
+def angles(by_frame, within, frame):
+    return [within[n] + by_frame[pl.ds(3 * frame + n, 1), :] for n in range(3)]
+
+
+def turn(z, angle, sign):
+    cosine, left, right = angle
     mixed = pltpu.roll(z, HEAD_DIM - 1, 1) * left + pltpu.roll(z, 1, 1) * right
     base = z * cosine
     return base + mixed if sign > 0 else base - mixed
@@ -104,13 +107,14 @@
     keep_s[...] = jnp.broadcast_to(mask[...].astype(F32), (FRAME_TOK, FRAME_TOK)).T
     keep = keep_s[pl.ds(pl.multiple_of(pl.program_id(0) * count, count), count), :] > 0.0
     rhos = [rho_of(raw) for raw in (query, key)]
+    angle = angles(by_frame, within, s)
     for k in range(GROUPS):
         for i, h in enumerate(heads):
             head = k * LOCAL_HEADS + h
             at = slice(head * HEAD_DIM, (head + 1) * HEAD_DIM)
             for n, (raw, gain) in enumerate(((query, gain_q), (key, gain_k))):
                 normed = raw[:, at].astype(F32) * rhos[n] * gain[head : head + 1, :]
-                outs[k, 4 * i + n] = turn(normed, by_frame, within, s, 1).astype(BF)
+                outs[k, 4 * i + n] = turn(normed, angle, 1).astype(BF)
             outs[k, 4 * i + 2] = value[:, at]
             outs[k, 4 * i + 3] = jnp.where(keep, cot[:, at].astype(F32), 0.0).astype(BF)
     if ups is None:
@@ -138,10 +142,15 @@
         outs[k, 4] = aux
 
 
-def attend_kernel(base, last, flags, packs, gain_q, gain_k, by_frame, within, ups, *refs):
-    before = None
+def attend_kernel(base, last, flags, packs, gain_q, gain_k, by_frame, *refs):
     if last:
-        before, refs = refs[0], refs[1:]
+        state, refs = refs[0], refs[1:]
+        before = state
+        within = [state[HELD + n * FRAME_TOK : HELD + (n + 1) * FRAME_TOK, :] for n in range(3)]
+        first = HELD + 3 * FRAME_TOK
+        ups = [state[first + n * RANK : first + (n + 1) * RANK, :].astype(BF) for n in range(3)]
+    else:
+        within, ups_all, *refs = refs
     wide_out, summed = refs[:2]
     refs = refs[2:]
     if last:
@@ -199,27 +208,36 @@
             dv_acc[...] += dv
             dk_acc[...] += dk
         dq_s[tile, :] = nn(kt_s[...], db[b]).T
-    up_at = pl.ds(pl.multiple_of(head * HEAD_DIM, HEAD_DIM), HEAD_DIM)
+    if not last:
+        up_at = pl.ds(pl.multiple_of(head * HEAD_DIM, HEAD_DIM), HEAD_DIM)
+        ups = [ups_all[n, :, up_at] for n in range(3)]
     gains = [gain[pl.ds(head, 1), :] for gain in (gain_q, gain_k)]
     for k in range(GROUPS):
         at = slice(k * FRAME_TOK, (k + 1) * FRAME_TOK)
+        angle = angles(by_frame, within, k)
         for n, (acc, rot) in enumerate(((dq_s, q_s), (dk_acc, k_s))):
             grad = (acc[at, :] * SCALING).astype(BF).astype(F32)
-            wide = gains[n] * turn(grad, by_frame, within, k, -1)
+            wide = gains[n] * turn(grad, angle, -1)
             wide_out[0, n, at, :] = wide.astype(BF)
             prod_s[n, at, :] = (grad * rot[at, :].astype(F32)).astype(BF)
         wide_out[0, 2, at, :] = dv_acc[at, :].astype(BF)
     ones = jnp.ones((16, HEAD_DIM), BF)
-    parts = [nt(ups[n, :, up_at], wide_out[0, n]) for n in range(3)]
+    parts = [nt(ups[n], wide_out[0, n]) for n in range(3)]
     parts += [nt(ones, prod_s[n])[0:8] for n in range(2)]
     full = jnp.concatenate(parts, 0)
     for k in range(GROUPS):
         part = full[:, k * FRAME_TOK : (k + 1) * FRAME_TOK]
+        at = slice(k * 112, (k + 1) * 112)
         if last:
-            sums[k] = part + before[k]
+            sums[k] = part + before[at, :]
         else:
-            summed[k] = part + jnp.where(step > 0, summed[k], 0.0)
+            summed[at, :] = part + jnp.where(step > 0, summed[at, :], 0.0)
     if not last:
+        later = pl.ds(pl.multiple_of((s * LOCAL_HEADS + 2) * HEAD_DIM, HEAD_DIM), HEAD_DIM)
+        for n in range(3):
+            summed[HELD + n * FRAME_TOK : HELD + (n + 1) * FRAME_TOK, :] = within[n]
+            first = HELD + 3 * FRAME_TOK + n * RANK
+            summed[first : first + RANK, :] = ups_all[n, :, later].astype(F32)
         return
     at_row = lax.broadcasted_iota(jnp.int32, (8, FRAME_TOK), 0)
     for n in range(2):
@@ -301,9 +319,10 @@
         lanes = slice(h * HEAD_DIM, (h + 1) * HEAD_DIM)
         for k in range(GROUPS):
             at = slice(k * FRAME_TOK, (k + 1) * FRAME_TOK)
+            angle = angles(by_frame, within, k)
             for n in range(2):
                 rot = (lasts if h == 2 else firsts)[k, 4 * (h % 2) + n].astype(F32)
-                turned_s[n, at, lanes] = turn(rot, by_frame, within, k, -1).astype(BF)
+                turned_s[n, at, lanes] = turn(rot, angle, -1).astype(BF)
     for n in range(3):
         plain_hi, plain_lo, along = [], [], []
         for p in range(GROUPS):
@@ -477,7 +496,7 @@
         extra += [shape((224, FRAME_TOK))] * 3
         out_specs += [VMEM] * 5
     else:
-        extra = [shape((GROUPS, 112, FRAME_TOK), F32)]
+        extra = [shape((HELD + 3 * FRAME_TOK + 96, FRAME_TOK), F32)]
         out_specs += [whole(a) for a in extra]
     return pl.pallas_call(
         functools.partial(attend_kernel, base, last),
@@ -501,7 +520,7 @@
             pltpu.VMEM((2, *rows), BF),
             pltpu.VMEM((GROUPS, 112, FRAME_TOK), F32),
         ],
-        compiler_params=params(BIG),
+        compiler_params=params(32),
         cost_estimate=pl.CostEstimate(
             flops=10 * heads * seq_len * seq_len * HEAD_DIM,
             bytes_accessed=heads * (4 << 20),
@@ -541,9 +560,8 @@
     )
     firsts = lax.all_to_all(firsts, "seq", 0, 0, tiled=True)
     lasts = lax.all_to_all(lasts, "seq", 0, 0, tiled=True)
-    shared = [*norms, adapter_up_maps]
-    wide01, before = attend(0, 2, [block_begin_flags, firsts, *shared], None)
-    wide2, kept, means, *mix = attend(2, 1, [block_begin_flags, lasts, *shared], before)
+    wide01, before = attend(0, 2, [block_begin_flags, firsts, *norms, adapter_up_maps], None)
+    wide2, kept, means, *mix = attend(2, 1, [block_begin_flags, lasts, *norms[:3]], before)
     mix = [swap(mix[a - 1], dy=a) for a in range(1, 4)]
     kept, means, mix = call(
         mix_kernel,

time: 149 us -> 145 us (0.973)
  Pallas kernels: 35 us -> 31.2 us
    pallas_call x2, Pallas kernels: 20 us -> 16.4 us  [attend(): pl.pallas_call(functools.partial(attend_kernel, base, last), grid=(heads,...]
    all_to_all x1, waiting for transfers between devices: 5.72 us -> 3.35 us  [shards(): lasts = lax.all_to_all(lasts, 'seq', 0, 0, tiled=True)]
    unnamed x28 -> x26, local copies, waits for them, and re-layouts: 4.05 us -> 5.16 us
  transfers between devices with their start and end apart: 26 -> 26, of which waited for: 18 -> 19; matrix products, arithmetic and copies ran while one was open for 0% -> 0% of each run, Pallas kernels for 14% -> 13%
where the time goes in v1:
time: 145 us
  starting transfers between devices  55.9 us (39%)
  waiting for transfers between devices  51.6 us (36%)
  Pallas kernels  31.2 us (22%)
  local copies, waits for them, and re-layouts  5.16 us (4%)
    ppermute x24, starting transfers between devices, swap(): return lax.ppermute(array, ('seq', 'dp'), pairs)  44.6 us
    ppermute x24, waiting for transfers between devices, swap(): return lax.ppermute(array, ('seq', 'dp'), pairs)  26.3 us
    all_to_all x1, waiting for transfers between devices, shards(): firsts = lax.all_to_all(firsts, 'seq', 0, 0, tiled=True)  21.9 us
    pallas_call x2, Pallas kernels, attend(): pl.pallas_call(functools.partial(attend_kernel, base, last), grid=(heads,...  16.4 us
    pallas_call x2, Pallas kernels, pack(): pl.pallas_call(functools.partial(pack_kernel, heads), grid=(steps,), out_...  10.8 us
    all_to_all x1, starting transfers between devices, shards(): firsts = lax.all_to_all(firsts, 'seq', 0, 0, tiled=True)  7.48 us
    unnamed x26, local copies, waits for them, and re-layouts  5.16 us
    pallas_call x12, Pallas kernels, call(): pl.pallas_call(kernel, out_shape=outs, in_specs=[SMEM] * smem + [VMEM] *...  4.06 us
  transfers between devices with their start and end apart: 26, of which 19 were waited for; matrix products, arithmetic and copies ran while one was open for 0% of the time, Pallas kernels for 13%

profile of v1, /device:TPU:1, one launch (start us, length us, event | category | flops | bytes accessed | tf_op | source)
XLA Modules:
  0.0 144.7 jit_solution(7261278749584672265)
XLA Ops:
  0.6 5.2 %shard_map.141 = bf16[8,8,128,128]{3,2,1,0:T(8,128)(2,1)} custom-call(bf16[128,3072]{1,0:T(8,128)(2,1)} %bitcast.23, bf16[128,3072]{1,0:T(8,128)(2,1)} %bitcast.25, bf16[128,3072]{1,0:T(8,128)(2,1)} %bitcast.27, bf16[128,3072]{1,0:T(8,128)(2,1)} %bitcast.29, s32[1,128]{1,0:T(1,128)} %bitcast.32, f32[24,128]{1,0:T(8,128)} %bitcast.13, f32[24,128]{1,0:T(8,128)} %bitcast.18, ...), custom_call_target="tpu_custom_call" | custom-call | tf_op jit(solution)/shard_map/pallas_call | solution.py:473
  5.8 7.5 %all-to-all-start.1 = ((bf16[8,8,128,128]{3,2,1,0:T(8,128)(2,1)}), bf16[8,8,128,128]{3,2,1,0:T(8,128)(2,1)S(1)}, u32[]{:S(2)}, u32[]{:S(2)}) async-start(bf16[8,8,128,128]{3,2,1,0:T(8,128)(2,1)} %shard_map.141), calls=%async_computation.1 | async-start | bytes 4194304 | tf_op jit(solution)/shard_map/all_to_all | solution.py:561
  13.3 5.6 %shard_map.140 = (bf16[8,5,128,128]{3,2,1,0:T(8,128)(2,1)}, f32[80,128]{1,0:T(8,128)}) custom-call(bf16[128,3072]{1,0:T(8,128)(2,1)} %bitcast.24, bf16[128,3072]{1,0:T(8,128)(2,1)} %bitcast.26, bf16[128,3072]{1,0:T(8,128)(2,1)} %bitcast.28, bf16[128,3072]{1,0:T(8,128)(2,1)} %bitcast.30, s32[1,128]{1,0:T(1,128)} %bitcast.33, f32[24,128]{1,0:T(8,128)} %bitcast.14, ...), custom_call_target="tpu_custom_call" | custom-call | tf_op jit(solution)/shard_map/pallas_call | solution.py:473
  18.9 21.9 %all-to-all-done.1.packs.firsts = bf16[8,8,128,128]{3,2,1,0:T(8,128)(2,1)S(1)} async-done(((bf16[8,8,128,128]{3,2,1,0:T(8,128)(2,1)}), bf16[8,8,128,128]{3,2,1,0:T(8,128)(2,1)S(1)}, u32[]{:S(2)}, u32[]{:S(2)}) %all-to-all-start.1) | async-done | bytes 2097184 | tf_op jit(solution)/shard_map/all_to_all | solution.py:561
  40.8 3.8 %all-to-all-start = ((bf16[8,5,128,128]{3,2,1,0:T(8,128)(2,1)}), bf16[8,5,128,128]{3,2,1,0:T(8,128)(2,1)S(1)}, u32[]{:S(2)}, u32[]{:S(2)}) async-start(bf16[8,5,128,128]{3,2,1,0:T(8,128)(2,1)} %get-tuple-element.32), calls=%async_computation | async-start | bytes 2621440 | tf_op jit(solution)/shard_map/all_to_all | solution.py:562
  44.7 0.9 copy-done.1
  45.6 1.1 copy-done.5
  46.7 10.7 %shard_map.142 = (bf16[2,3,1024,128]{3,2,1,0:T(8,128)(2,1)S(1)}, f32[1376,128]{1,0:T(8,128)S(1)}) custom-call(s32[1,8]{1,0:T(1,128)S(1)} %copy-done.10, bf16[8,8,128,128]{3,2,1,0:T(8,128)(2,1)S(1)} %all-to-all-done.1.packs.firsts, f32[24,128]{1,0:T(8,128)S(1)} %bitcast.15, f32[24,128]{1,0:T(8,128)S(1)} %bitcast.20, f32[24,128]{1,0:T(8,128)S(1)} %copy-done.8, ...), custom_call_target="tpu_custom_call" | custom-call | flops 2684354560 | bytes 8388608 | tf_op jit(solution)/shard_map/pallas_call | solution.py:501
  57.4 1.2 copy-done.3
  58.6 0.8 copy-done.11
  59.5 3.4 %all-to-all-done.packs.lasts = bf16[8,5,128,128]{3,2,1,0:T(8,128)(2,1)S(1)} async-done(((bf16[8,5,128,128]{3,2,1,0:T(8,128)(2,1)}), bf16[8,5,128,128]{3,2,1,0:T(8,128)(2,1)S(1)}, u32[]{:S(2)}, u32[]{:S(2)}) %all-to-all-start) | async-done | bytes 1310752 | tf_op jit(solution)/shard_map/all_to_all | solution.py:562
  62.8 1.1 copy-done.12
  63.9 5.6 %shard_map.143 = (bf16[1,3,1024,128]{3,2,1,0:T(8,128)(2,1)S(1)}, f32[2,96,128]{2,1,0:T(8,128)S(1)}, f32[16,128]{1,0:T(8,128)S(1)}, bf16[224,128]{1,0:T(8,128)(2,...) custom-call(s32[1,8]{1,0:T(1,128)S(1)} %copy-done.10, ...), custom_call_target="tpu_custom_call" | custom-call | flops 1342177280 | bytes 4194304 | tf_op jit(solution)/shard_map/pallas_call | solution.py:501
  69.9 2.1 %collective-permute-start.1 = (bf16[224,128]{1,0:T(8,128)(2,1)S(1)}, bf16[224,128]{1,0:T(8,128)(2,1)S(1)}, u32[]{:S(2)}, u32[]{:S(2)}) collective-permute-start(bf16[224,128]{1,0:T(8,128)(2,1)S(1)} %get-tuple-element.37), channel_id=1, source_target_pairs={{0,128},{1,129},{4,132},{5,133},{8,136},{9,137},{12,140},{13,141},... | collective-permute-start | bytes 172040 | tf_op jit(solution)/shard_map/ppermute | solution.py:455
  71.9 1.8 %collective-permute-start.2 = (bf16[224,128]{1,0:T(8,128)(2,1)S(1)}, bf16[224,128]{1,0:T(8,128)(2,1)S(1)}, u32[]{:S(2)}, u32[]{:S(2)}) collective-permute-start(bf16[224,128]{1,0:T(8,128)(2,1)S(1)} %get-tuple-element.38), channel_id=1, source_target_pairs={{0,192},{1,193},{4,196},{5,197},{8,200},{9,201},{12,204},{13,205},... | collective-permute-start | bytes 172040 | tf_op jit(solution)/shard_map/ppermute | solution.py:455
  73.7 0.8 collective-permute-done.1.r2
  74.5 1.7 %collective-permute-done.2.r3 = bf16[224,128]{1,0:T(8,128)(2,1)S(1)} collective-permute-done((bf16[224,128]{1,0:T(8,128)(2,1)S(1)}, bf16[224,128]{1,0:T(8,128)(2,1)S(1)}, u32[]{:S(2)}, u32[]{:S(2)}) %collective-permute-start.2) | collective-permute-done | bytes 57376 | tf_op jit(solution)/shard_map/ppermute | solution.py:455
  76.2 3.3 %collective-permute-start.3 = (bf16[128,128]{1,0:T(8,128)(2,1)S(1)}, bf16[128,128]{1,0:T(8,128)(2,1)S(1)}, u32[]{:S(2)}, u32[]{:S(2)}) collective-permute-start(bf16[128,128]{1,0:T(8,128)(2,1)S(1)} %get-tuple-element.41), channel_id=1, source_target_pairs={{0,32},{1,33},{4,36},{5,37},{8,40},{9,41},{12,44},{13,45},{16,48},... | collective-permute-start | bytes 98312 | tf_op jit(solution)/shard_map/ppermute | solution.py:455
  79.5 1.3 collective-permute-done.3.got
  80.8 0.4 shard_map.145
  81.3 5.2 %collective-permute-start.4 = (bf16[4,4,24,640]{3,2,1,0:T(8,128)(2,1)S(1)}, bf16[4,4,24,640]{3,2,1,0:T(8,128)(2,1)S(1)}, u32[]{:S(2)}, u32[]{:S(2)}) collective-permute-start(bf16[4,4,24,640]{3,2,1,0:T(8,128)(2,1)S(1)} %get-tuple-element.44), channel_id=1, source_target_pairs={{0,1},{1,0},{4,5},{5,4},{8,9},{9,8},{12,13},{13,12},{16,17},{17,16... | collective-permute-start | bytes 1474568 | tf_op jit(solution)/shard_map/ppermute | solution.py:455
  86.5 1.5 %collective-permute-done.4.got = bf16[4,4,24,640]{3,2,1,0:T(8,128)(2,1)S(1)} collective-permute-done((bf16[4,4,24,640]{3,2,1,0:T(8,128)(2,1)S(1)}, bf16[4,4,24,640]{3,2,1,0:T(8,128)(2,1)S(1)}, u32[]{:S(2)}, u32[]{:S(2)}) %collective-permute-start.4) | collective-permute-done | bytes 491552 | tf_op jit(solution)/shard_map/ppermute | solution.py:455
  88.0 0.4 collective-permute-start.5
  88.4 1.5 %collective-permute-start.6 = (bf16[4,24,640]{2,1,0:T(8,128)(2,1)S(1)}, bf16[4,24,640]{2,1,0:T(8,128)(2,1)S(1)}, u32[]{:S(2)}, u32[]{:S(2)}) collective-permute-start(bf16[4,24,640]{2,1,0:T(8,128)(2,1)S(1)} %get-tuple-element.47), channel_id=1, source_target_pairs={{0,32},{1,33},{4,36},{5,37},{8,40},{9,41},{12,44},{13,45},{16,48},... | collective-permute-start | bytes 368648 | tf_op jit(solution)/shard_map/ppermute | solution.py:455
  89.9 2.1 %collective-permute-start.7 = (bf16[4,24,640]{2,1,0:T(8,128)(2,1)S(1)}, bf16[4,24,640]{2,1,0:T(8,128)(2,1)S(1)}, u32[]{:S(2)}, u32[]{:S(2)}) collective-permute-start(bf16[4,24,640]{2,1,0:T(8,128)(2,1)S(1)} %get-tuple-element.48), channel_id=1, source_target_pairs={{0,34},{1,35},{4,38},{5,39},{8,42},{9,43},{12,46},{13,47},{16,50},... | collective-permute-start | bytes 368648 | tf_op jit(solution)/shard_map/ppermute | solution.py:455
  92.0 1.9 %shard_map.148 = (f32[2,24,384]{2,1,0:T(8,128)S(1)}, bf16[2,24,384]{2,1,0:T(8,128)(2,1)S(1)}) custom-call(f32[16,128]{1,0:T(8,128)S(1)} %get-tuple-element.53.means, bf16[8,8,128,128]{3,2,1,0:T(8,128)(2,1)S(1)} %all-to-all-done.1.packs.firsts, bf16[8,5,128,128]{3,2,1,0:T(8,128)(2,1)S(1)} %all-to-all-done.packs.lasts, ...), custom_call_target="tpu_custom_call" | custom-call | tf_op jit(solution)/shard_map/pallas_call | solution.py:433
  93.9 1.3 collective-permute-start.11
  95.2 0.5 collective-permute-done.6.r2
  95.7 2.5 %collective-permute-done.7.r3 = bf16[4,24,640]{2,1,0:T(8,128)(2,1)S(1)} collective-permute-done((bf16[4,24,640]{2,1,0:T(8,128)(2,1)S(1)}, bf16[4,24,640]{2,1,0:T(8,128)(2,1)S(1)}, u32[]{:S(2)}, u32[]{:S(2)}) %collective-permute-start.7) | collective-permute-done | bytes 122912 | tf_op jit(solution)/shard_map/ppermute | solution.py:455
  98.4 3.0 %collective-permute-start.9 = (bf16[24,640]{1,0:T(8,128)(2,1)S(1)}, bf16[24,640]{1,0:T(8,128)(2,1)S(1)}, u32[]{:S(2)}, u32[]{:S(2)}) collective-permute-start(bf16[24,640]{1,0:T(8,128)(2,1)S(1)} %get-tuple-element.51), channel_id=1, source_target_pairs={{0,128},{1,129},{4,132},{5,133},{8,136},{9,137},{12,140},{13,141},... | collective-permute-start | bytes 92168 | tf_op jit(solution)/shard_map/ppermute | solution.py:455
  101.3 0.9 collective-permute-start.10
  102.3 2.6 %collective-permute-done.12.up_got = bf16[24,384]{1,0:T(8,128)(2,1)S(1)} collective-permute-done((bf16[24,384]{1,0:T(8,128)(2,1)S(1)}, bf16[24,384]{1,0:T(8,128)(2,1)S(1)}, u32[]{:S(2)}, u32[]{:S(2)}) %collective-permute-start.12) | collective-permute-done | bytes 18464 | tf_op jit(solution)/shard_map/ppermute | solution.py:455
  105.3 4.4 %collective-permute-start.15 = (bf16[24,1024]{1,0:T(8,128)(2,1)S(1)}, bf16[24,1024]{1,0:T(8,128)(2,1)S(1)}, u32[]{:S(2)}, u32[]{:S(2)}) collective-permute-start(bf16[24,1024]{1,0:T(8,128)(2,1)S(1)} %shard_map.150.own), channel_id=1, source_target_pairs={{0,12},{1,13},{4,8},{5,9},{8,4},{9,5},{12,0},{13,1},{16,28},{17,29... | collective-permute-start | bytes 147464 | tf_op jit(solution)/shard_map/ppermute | solution.py:455
  110.1 1.1 collective-permute-done.15.r3
  111.2 2.7 %collective-permute-done.14.r2 = bf16[24,1024]{1,0:T(8,128)(2,1)S(1)} collective-permute-done((bf16[24,1024]{1,0:T(8,128)(2,1)S(1)}, bf16[24,1024]{1,0:T(8,128)(2,1)S(1)}, u32[]{:S(2)}, u32[]{:S(2)}) %collective-permute-start.14) | collective-permute-done | bytes 49184 | tf_op jit(solution)/shard_map/ppermute | solution.py:455
  113.9 3.0 %collective-permute-start.16 = (bf16[24,1024]{1,0:T(8,128)(2,1)S(1)}, bf16[24,1024]{1,0:T(8,128)(2,1)S(1)}, u32[]{:S(2)}, u32[]{:S(2)}) collective-permute-start(bf16[24,1024]{1,0:T(8,128)(2,1)S(1)} %shard_map.151.own), channel_id=1, source_target_pairs={{0,28},{1,29},{4,24},{5,25},{8,20},{9,21},{12,16},{13,17},{16,12},... | collective-permute-start | bytes 147464 | tf_op jit(solution)/shard_map/ppermute | solution.py:455
  116.9 1.5 %collective-permute-done.16.got = bf16[24,1024]{1,0:T(8,128)(2,1)S(1)} collective-permute-done((bf16[24,1024]{1,0:T(8,128)(2,1)S(1)}, bf16[24,1024]{1,0:T(8,128)(2,1)S(1)}, u32[]{:S(2)}, u32[]{:S(2)}) %collective-permute-start.16) | collective-permute-done | bytes 49184 | tf_op jit(solution)/shard_map/ppermute | solution.py:455
  118.4 1.7 %collective-permute-start.19 = (bf16[24,1024]{1,0:T(8,128)(2,1)S(1)}, bf16[24,1024]{1,0:T(8,128)(2,1)S(1)}, u32[]{:S(2)}, u32[]{:S(2)}) collective-permute-start(bf16[24,1024]{1,0:T(8,128)(2,1)S(1)} %shard_map.152.refs_0_), channel_id=1, source_target_pairs={{0,192},{1,193},{4,196},{5,197},{8,200},{9,201},{12,204},{13,205},... | collective-permute-start | bytes 147464 | tf_op jit(solution)/shard_map/ppermute | solution.py:455
  120.0 1.7 %collective-permute-start.17 = (bf16[24,1024]{1,0:T(8,128)(2,1)S(1)}, bf16[24,1024]{1,0:T(8,128)(2,1)S(1)}, u32[]{:S(2)}, u32[]{:S(2)}) collective-permute-start(bf16[24,1024]{1,0:T(8,128)(2,1)S(1)} %shard_map.152.refs_0_), channel_id=1, source_target_pairs={{0,64},{1,65},{4,68},{5,69},{8,72},{9,73},{12,76},{13,77},{16,80},... | collective-permute-start | bytes 147464 | tf_op jit(solution)/shard_map/ppermute | solution.py:455
  121.7 1.2 collective-permute-done.19.refs_3_
  122.9 1.6 %collective-permute-done.18.refs_2_ = bf16[24,1024]{1,0:T(8,128)(2,1)S(1)} collective-permute-done((bf16[24,1024]{1,0:T(8,128)(2,1)S(1)}, bf16[24,1024]{1,0:T(8,128)(2,1)S(1)}, u32[]{:S(2)}, u32[]{:S(2)}) %collective-permute-start.18) | collective-permute-done | bytes 49184 | tf_op jit(solution)/shard_map/ppermute | solution.py:455
  124.5 2.4 %collective-permute-start.22 = (bf16[4,24,1024]{2,1,0:T(8,128)(2,1)S(1)}, bf16[4,24,1024]{2,1,0:T(8,128)(2,1)S(1)}, u32[]{:S(2)}, u32[]{:S(2)}) collective-permute-start(bf16[4,24,1024]{2,1,0:T(8,128)(2,1)S(1)} %shard_map.153.refs_0_), channel_id=1, source_target_pairs={{0,34},{1,35},{4,38},{5,39},{8,42},{9,43},{12,46},{13,47},{16,50},... | collective-permute-start | bytes 589832 | tf_op jit(solution)/shard_map/ppermute | solution.py:455
  127.1 0.7 collective-permute-start.20
  127.8 3.8 %collective-permute-done.22.refs_3_ = bf16[4,24,1024]{2,1,0:T(8,128)(2,1)S(1)} collective-permute-done((bf16[4,24,1024]{2,1,0:T(8,128)(2,1)S(1)}, bf16[4,24,1024]{2,1,0:T(8,128)(2,1)S(1)}, u32[]{:S(2)}, u32[]{:S(2)}) %collective-permute-start.22) | collective-permute-done | bytes 196640 | tf_op jit(solution)/shard_map/ppermute | solution.py:455
  131.7 1.3 collective-permute-done.21.refs_2_
  133.1 8.3 %collective-permute-start.23 = (bf16[4,4,24,1024]{3,2,1,0:T(8,128)(2,1)S(1)}, bf16[4,4,24,1024]{3,2,1,0:T(8,128)(2,1)S(1)}, u32[]{:S(2)}, u32[]{:S(2)}) collective-permute-start(bf16[4,4,24,1024]{3,2,1,0:T(8,128)(2,1)S(1)} %shard_map.154.own), channel_id=1, source_target_pairs={{0,1},{1,0},{4,5},{5,4},{8,9},{9,8},{12,13},{13,12},{16,17},{17,16... | collective-permute-start | bytes 2359304 | tf_op jit(solution)/shard_map/ppermute | solution.py:455
  141.4 1.9 %collective-permute-done.23.got = bf16[4,4,24,1024]{3,2,1,0:T(8,128)(2,1)S(1)} collective-permute-done((bf16[4,4,24,1024]{3,2,1,0:T(8,128)(2,1)S(1)}, bf16[4,4,24,1024]{3,2,1,0:T(8,128)(2,1)S(1)}, u32[]{:S(2)}, u32[]{:S(2)}) %collective-permute-start.23) | collective-permute-done | bytes 786464 | tf_op jit(solution)/shard_map/ppermute | solution.py:455
  143.3 1.4 shard_map.155
  (46 shorter events, 1.8 us)
Async XLA Ops:
  5.8 35.0 %all-to-all-start.1 = ((bf16[8,8,128,128]{3,2,1,0:T(8,128)(2,1)}), bf16[8,8,128,128]{3,2,1,0:T(8,128)(2,1)S(1)}, u32[]{:S(2)}, u32[]{:S(2)}) async-start(bf16[8,8,128,128]{3,2,1,0:T(8,128)(2,1)} %shard_map.141), calls=%async_computation.1 | async-start | bytes 4194304 | tf_op jit(solution)/shard_map/all_to_all | solution.py:561
  18.9 25.8 %copy-start.6 = (f32[3072]{0:T(1024)S(1)}, f32[3072]{0:T(1024)}, u32[]{:S(2)}) copy-start(f32[3072]{0:T(1024)} %param.18) | copy-start | bytes 36868
  18.9 25.8 %copy-start.7 = (f32[3072]{0:T(1024)S(1)}, f32[3072]{0:T(1024)}, u32[]{:S(2)}) copy-start(f32[3072]{0:T(1024)} %param.19) | copy-start | bytes 36868
  18.9 25.8 %copy-start.8 = (f32[24,128]{1,0:T(8,128)S(1)}, f32[24,128]{1,0:T(8,128)}, u32[]{:S(2)}) copy-start(f32[24,128]{1,0:T(8,128)} %constant.4.clone.by_frame.refs_2_) | copy-start | bytes 36868
  18.9 25.8 %copy-start.10 = (s32[1,8]{1,0:T(1,128)S(1)}, s32[1,8]{1,0:T(1,128)}, u32[]{:S(2)}) copy-start(s32[1,8]{1,0:T(1,128)} %flags.3) | copy-start | bytes 100
  40.8 22.0 %all-to-all-start = ((bf16[8,5,128,128]{3,2,1,0:T(8,128)(2,1)}), bf16[8,5,128,128]{3,2,1,0:T(8,128)(2,1)S(1)}, u32[]{:S(2)}, u32[]{:S(2)}) async-start(bf16[8,5,128,128]{3,2,1,0:T(8,128)(2,1)} %get-tuple-element.32), calls=%async_computation | async-start | bytes 2621440 | tf_op jit(solution)/shard_map/all_to_all | solution.py:562
  44.7 0.9 copy-start.1
  45.6 1.1 copy-start.5
  57.4 1.2 copy-start.3
  58.6 0.9 copy-start.11
  62.8 1.1 copy-start.12
  63.9 16.9 %copy-start = (bf16[1,128,5120]{2,1,0:T(8,128)(2,1)S(1)}, bf16[1,128,5120]{2,1,0:T(8,128)(2,1)}, u32[]{:S(2)}) copy-start(bf16[1,128,5120]{2,1,0:T(8,128)(2,1)} %param.13) | copy-start | bytes 3932164
  63.9 16.9 %copy-start.9 = (f32[80,128]{1,0:T(8,128)S(1)}, f32[80,128]{1,0:T(8,128)}, u32[]{:S(2)}) copy-start(f32[80,128]{1,0:T(8,128)} %get-tuple-element.42.local) | copy-start | bytes 122884
  69.6 4.1 %collective-permute-start = (bf16[224,128]{1,0:T(8,128)(2,1)S(1)}, bf16[224,128]{1,0:T(8,128)(2,1)S(1)}, u32[]{:S(2)}, u32[]{:S(2)}) collective-permute-start(bf16[224,128]{1,0:T(8,128)(2,1)S(1)} %get-tuple-element.36), channel_id=1, source_target_pairs={{0,64},{1,65},{4,68},{5,69},{8,72},{9,73},{12,76},{13,77},{16,80},... | collective-permute-start | bytes 172040 | tf_op jit(solution)/shard_map/ppermute | solution.py:455
  69.9 4.6 %collective-permute-start.1 = (bf16[224,128]{1,0:T(8,128)(2,1)S(1)}, bf16[224,128]{1,0:T(8,128)(2,1)S(1)}, u32[]{:S(2)}, u32[]{:S(2)}) collective-permute-start(bf16[224,128]{1,0:T(8,128)(2,1)S(1)} %get-tuple-element.37), channel_id=1, source_target_pairs={{0,128},{1,129},{4,132},{5,133},{8,136},{9,137},{12,140},{13,141},... | collective-permute-start | bytes 172040 | tf_op jit(solution)/shard_map/ppermute | solution.py:455
  71.9 4.2 %collective-permute-start.2 = (bf16[224,128]{1,0:T(8,128)(2,1)S(1)}, bf16[224,128]{1,0:T(8,128)(2,1)S(1)}, u32[]{:S(2)}, u32[]{:S(2)}) collective-permute-start(bf16[224,128]{1,0:T(8,128)(2,1)S(1)} %get-tuple-element.38), channel_id=1, source_target_pairs={{0,192},{1,193},{4,196},{5,197},{8,200},{9,201},{12,204},{13,205},... | collective-permute-start | bytes 172040 | tf_op jit(solution)/shard_map/ppermute | solution.py:455
  76.2 15.8 %copy-start.2 = (f32[3,128,128]{2,1,0:T(8,128)S(1)}, f32[3,128,128]{2,1,0:T(8,128)}, u32[]{:S(2)}) copy-start(f32[3,128,128]{2,1,0:T(8,128)} %constant.5.clone.within.refs_0_.refs_3_) | copy-start | bytes 589828
  76.2 15.8 %copy-start.4 = (bf16[2,3,1024,128]{3,2,1,0:T(8,128)(2,1)S(1)}, bf16[2,3,1024,128]{3,2,1,0:T(8,128)(2,1)}, u32[]{:S(2)}) copy-start(bf16[2,3,1024,128]{3,2,1,0:T(8,128)(2,1)} %copy-done.3) | copy-start | bytes 4718596
  76.2 4.6 %collective-permute-start.3 = (bf16[128,128]{1,0:T(8,128)(2,1)S(1)}, bf16[128,128]{1,0:T(8,128)(2,1)S(1)}, u32[]{:S(2)}, u32[]{:S(2)}) collective-permute-start(bf16[128,128]{1,0:T(8,128)(2,1)S(1)} %get-tuple-element.41), channel_id=1, source_target_pairs={{0,32},{1,33},{4,36},{5,37},{8,40},{9,41},{12,44},{13,45},{16,48},... | collective-permute-start | bytes 98312 | tf_op jit(solution)/shard_map/ppermute | solution.py:455
  81.3 6.7 %collective-permute-start.4 = (bf16[4,4,24,640]{3,2,1,0:T(8,128)(2,1)S(1)}, bf16[4,4,24,640]{3,2,1,0:T(8,128)(2,1)S(1)}, u32[]{:S(2)}, u32[]{:S(2)}) collective-permute-start(bf16[4,4,24,640]{3,2,1,0:T(8,128)(2,1)S(1)} %get-tuple-element.44), channel_id=1, source_target_pairs={{0,1},{1,0},{4,5},{5,4},{8,9},{9,8},{12,13},{13,12},{16,17},{17,16... | collective-permute-start | bytes 1474568 | tf_op jit(solution)/shard_map/ppermute | solution.py:455
  88.0 7.1 %collective-permute-start.5 = (bf16[4,24,640]{2,1,0:T(8,128)(2,1)S(1)}, bf16[4,24,640]{2,1,0:T(8,128)(2,1)S(1)}, u32[]{:S(2)}, u32[]{:S(2)}) collective-permute-start(bf16[4,24,640]{2,1,0:T(8,128)(2,1)S(1)} %get-tuple-element.46), channel_id=1, source_target_pairs={{0,2},{1,3},{4,6},{5,7},{8,10},{9,11},{12,14},{13,15},{16,18},{17,... | collective-permute-start | bytes 368648 | tf_op jit(solution)/shard_map/ppermute | solution.py:455
  88.4 7.2 %collective-permute-start.6 = (bf16[4,24,640]{2,1,0:T(8,128)(2,1)S(1)}, bf16[4,24,640]{2,1,0:T(8,128)(2,1)S(1)}, u32[]{:S(2)}, u32[]{:S(2)}) collective-permute-start(bf16[4,24,640]{2,1,0:T(8,128)(2,1)S(1)} %get-tuple-element.47), channel_id=1, source_target_pairs={{0,32},{1,33},{4,36},{5,37},{8,40},{9,41},{12,44},{13,45},{16,48},... | collective-permute-start | bytes 368648 | tf_op jit(solution)/shard_map/ppermute | solution.py:455
  89.9 8.2 %collective-permute-start.7 = (bf16[4,24,640]{2,1,0:T(8,128)(2,1)S(1)}, bf16[4,24,640]{2,1,0:T(8,128)(2,1)S(1)}, u32[]{:S(2)}, u32[]{:S(2)}) collective-permute-start(bf16[4,24,640]{2,1,0:T(8,128)(2,1)S(1)} %get-tuple-element.48), channel_id=1, source_target_pairs={{0,34},{1,35},{4,38},{5,39},{8,42},{9,43},{12,46},{13,47},{16,50},... | collective-permute-start | bytes 368648 | tf_op jit(solution)/shard_map/ppermute | solution.py:455
  93.9 8.3 %collective-permute-start.11 = (bf16[2,24,384]{2,1,0:T(8,128)(2,1)S(1)}, bf16[2,24,384]{2,1,0:T(8,128)(2,1)S(1)}, u32[]{:S(2)}, u32[]{:S(2)}) collective-permute-start(bf16[2,24,384]{2,1,0:T(8,128)(2,1)S(1)} %get-tuple-element.57), channel_id=1, source_target_pairs={{0,1},{1,0},{4,5},{5,4},{8,9},{9,8},{12,13},{13,12},{16,17},{17,16... | collective-permute-start | bytes 110600 | tf_op jit(solution)/shard_map/ppermute | solution.py:455
  98.3 6.7 %collective-permute-start.8 = (bf16[24,640]{1,0:T(8,128)(2,1)S(1)}, bf16[24,640]{1,0:T(8,128)(2,1)S(1)}, u32[]{:S(2)}, u32[]{:S(2)}) collective-permute-start(bf16[24,640]{1,0:T(8,128)(2,1)S(1)} %get-tuple-element.50), channel_id=1, source_target_pairs={{0,64},{1,65},{4,68},{5,69},{8,72},{9,73},{12,76},{13,77},{16,80},... | collective-permute-start | bytes 92168 | tf_op jit(solution)/shard_map/ppermute | solution.py:455
  98.4 6.6 %collective-permute-start.9 = (bf16[24,640]{1,0:T(8,128)(2,1)S(1)}, bf16[24,640]{1,0:T(8,128)(2,1)S(1)}, u32[]{:S(2)}, u32[]{:S(2)}) collective-permute-start(bf16[24,640]{1,0:T(8,128)(2,1)S(1)} %get-tuple-element.51), channel_id=1, source_target_pairs={{0,128},{1,129},{4,132},{5,133},{8,136},{9,137},{12,140},{13,141},... | collective-permute-start | bytes 92168 | tf_op jit(solution)/shard_map/ppermute | solution.py:455
  101.3 4.0 %collective-permute-start.10 = (bf16[24,640]{1,0:T(8,128)(2,1)S(1)}, bf16[24,640]{1,0:T(8,128)(2,1)S(1)}, u32[]{:S(2)}, u32[]{:S(2)}) collective-permute-start(bf16[24,640]{1,0:T(8,128)(2,1)S(1)} %get-tuple-element.52), channel_id=1, source_target_pairs={{0,192},{1,193},{4,196},{5,197},{8,200},{9,201},{12,204},{13,205},... | collective-permute-start | bytes 92168 | tf_op jit(solution)/shard_map/ppermute | solution.py:455
  102.2 2.7 %collective-permute-start.12 = (bf16[24,384]{1,0:T(8,128)(2,1)S(1)}, bf16[24,384]{1,0:T(8,128)(2,1)S(1)}, u32[]{:S(2)}, u32[]{:S(2)}) collective-permute-start(bf16[24,384]{1,0:T(8,128)(2,1)S(1)} %get-tuple-element.59), channel_id=1, source_target_pairs={{0,2},{1,3},{4,6},{5,7},{8,10},{9,11},{12,14},{13,15},{16,18},{17,... | collective-permute-start | bytes 55304 | tf_op jit(solution)/shard_map/ppermute | solution.py:455
  105.3 5.9 %collective-permute-start.15 = (bf16[24,1024]{1,0:T(8,128)(2,1)S(1)}, bf16[24,1024]{1,0:T(8,128)(2,1)S(1)}, u32[]{:S(2)}, u32[]{:S(2)}) collective-permute-start(bf16[24,1024]{1,0:T(8,128)(2,1)S(1)} %shard_map.150.own), channel_id=1, source_target_pairs={{0,12},{1,13},{4,8},{5,9},{8,4},{9,5},{12,0},{13,1},{16,28},{17,29... | collective-permute-start | bytes 147464 | tf_op jit(solution)/shard_map/ppermute | solution.py:455
  109.7 4.1 %collective-permute-start.14 = (bf16[24,1024]{1,0:T(8,128)(2,1)S(1)}, bf16[24,1024]{1,0:T(8,128)(2,1)S(1)}, u32[]{:S(2)}, u32[]{:S(2)}) collective-permute-start(bf16[24,1024]{1,0:T(8,128)(2,1)S(1)} %shard_map.150.own), channel_id=1, source_target_pairs={{0,8},{1,9},{4,12},{5,13},{8,0},{9,1},{12,4},{13,5},{16,24},{17,25... | collective-permute-start | bytes 147464 | tf_op jit(solution)/shard_map/ppermute | solution.py:455
  109.7 4.1 %collective-permute-start.13 = (bf16[24,1024]{1,0:T(8,128)(2,1)S(1)}, bf16[24,1024]{1,0:T(8,128)(2,1)S(1)}, u32[]{:S(2)}, u32[]{:S(2)}) collective-permute-start(bf16[24,1024]{1,0:T(8,128)(2,1)S(1)} %shard_map.150.own), channel_id=1, source_target_pairs={{0,4},{1,5},{4,0},{5,1},{8,12},{9,13},{12,8},{13,9},{16,20},{17,21... | collective-permute-start | bytes 147464 | tf_op jit(solution)/shard_map/ppermute | solution.py:455
  113.9 4.4 %collective-permute-start.16 = (bf16[24,1024]{1,0:T(8,128)(2,1)S(1)}, bf16[24,1024]{1,0:T(8,128)(2,1)S(1)}, u32[]{:S(2)}, u32[]{:S(2)}) collective-permute-start(bf16[24,1024]{1,0:T(8,128)(2,1)S(1)} %shard_map.151.own), channel_id=1, source_target_pairs={{0,28},{1,29},{4,24},{5,25},{8,20},{9,21},{12,16},{13,17},{16,12},... | collective-permute-start | bytes 147464 | tf_op jit(solution)/shard_map/ppermute | solution.py:455
  118.4 4.5 %collective-permute-start.19 = (bf16[24,1024]{1,0:T(8,128)(2,1)S(1)}, bf16[24,1024]{1,0:T(8,128)(2,1)S(1)}, u32[]{:S(2)}, u32[]{:S(2)}) collective-permute-start(bf16[24,1024]{1,0:T(8,128)(2,1)S(1)} %shard_map.152.refs_0_), channel_id=1, source_target_pairs={{0,192},{1,193},{4,196},{5,197},{8,200},{9,201},{12,204},{13,205},... | collective-permute-start | bytes 147464 | tf_op jit(solution)/shard_map/ppermute | solution.py:455
  120.0 4.4 %collective-permute-start.18 = (bf16[24,1024]{1,0:T(8,128)(2,1)S(1)}, bf16[24,1024]{1,0:T(8,128)(2,1)S(1)}, u32[]{:S(2)}, u32[]{:S(2)}) collective-permute-start(bf16[24,1024]{1,0:T(8,128)(2,1)S(1)} %shard_map.152.refs_0_), channel_id=1, source_target_pairs={{0,128},{1,129},{4,132},{5,133},{8,136},{9,137},{12,140},{13,141},... | collective-permute-start | bytes 147464 | tf_op jit(solution)/shard_map/ppermute | solution.py:455
  120.0 4.4 %collective-permute-start.17 = (bf16[24,1024]{1,0:T(8,128)(2,1)S(1)}, bf16[24,1024]{1,0:T(8,128)(2,1)S(1)}, u32[]{:S(2)}, u32[]{:S(2)}) collective-permute-start(bf16[24,1024]{1,0:T(8,128)(2,1)S(1)} %shard_map.152.refs_0_), channel_id=1, source_target_pairs={{0,64},{1,65},{4,68},{5,69},{8,72},{9,73},{12,76},{13,77},{16,80},... | collective-permute-start | bytes 147464 | tf_op jit(solution)/shard_map/ppermute | solution.py:455
  124.5 7.2 %collective-permute-start.22 = (bf16[4,24,1024]{2,1,0:T(8,128)(2,1)S(1)}, bf16[4,24,1024]{2,1,0:T(8,128)(2,1)S(1)}, u32[]{:S(2)}, u32[]{:S(2)}) collective-permute-start(bf16[4,24,1024]{2,1,0:T(8,128)(2,1)S(1)} %shard_map.153.refs_0_), channel_id=1, source_target_pairs={{0,34},{1,35},{4,38},{5,39},{8,42},{9,43},{12,46},{13,47},{16,50},... | collective-permute-start | bytes 589832 | tf_op jit(solution)/shard_map/ppermute | solution.py:455
  126.9 6.0 %collective-permute-start.21 = (bf16[4,24,1024]{2,1,0:T(8,128)(2,1)S(1)}, bf16[4,24,1024]{2,1,0:T(8,128)(2,1)S(1)}, u32[]{:S(2)}, u32[]{:S(2)}) collective-permute-start(bf16[4,24,1024]{2,1,0:T(8,128)(2,1)S(1)} %shard_map.153.refs_0_), channel_id=1, source_target_pairs={{0,32},{1,33},{4,36},{5,37},{8,40},{9,41},{12,44},{13,45},{16,48},... | collective-permute-start | bytes 589832 | tf_op jit(solution)/shard_map/ppermute | solution.py:455
  127.1 5.9 %collective-permute-start.20 = (bf16[4,24,1024]{2,1,0:T(8,128)(2,1)S(1)}, bf16[4,24,1024]{2,1,0:T(8,128)(2,1)S(1)}, u32[]{:S(2)}, u32[]{:S(2)}) collective-permute-start(bf16[4,24,1024]{2,1,0:T(8,128)(2,1)S(1)} %shard_map.153.refs_0_), channel_id=1, source_target_pairs={{0,2},{1,3},{4,6},{5,7},{8,10},{9,11},{12,14},{13,15},{16,18},{17,... | collective-permute-start | bytes 589832 | tf_op jit(solution)/shard_map/ppermute | solution.py:455
  133.1 10.2 %collective-permute-start.23 = (bf16[4,4,24,1024]{3,2,1,0:T(8,128)(2,1)S(1)}, bf16[4,4,24,1024]{3,2,1,0:T(8,128)(2,1)S(1)}, u32[]{:S(2)}, u32[]{:S(2)}) collective-permute-start(bf16[4,4,24,1024]{3,2,1,0:T(8,128)(2,1)S(1)} %shard_map.154.own), channel_id=1, source_target_pairs={{0,1},{1,0},{4,5},{5,4},{8,9},{9,8},{12,13},{13,12},{16,17},{17,16... | collective-permute-start | bytes 2359304 | tf_op jit(solution)/shard_map/ppermute | solution.py:455

commit v2 on v1

--- a/solution.py
+++ b/solution.py
@@ -102,7 +102,10 @@
 
 def pack_kernel(heads, query, key, value, cot, mask, gain_q, gain_k, by_frame, within, *refs):
     s = lax.axis_index("seq")
-    ups, downs, tokens, outs, local, keep_s = refs if len(refs) > 2 else (None,) * 3 + (refs[0], None, refs[1])
+    if len(refs) > 2:
+        ups, downs, tokens, *outs, local, keep_s = refs
+    else:
+        ups, (outs, keep_s) = None, refs
     count = query.shape[0]
     keep_s[...] = jnp.broadcast_to(mask[...].astype(F32), (FRAME_TOK, FRAME_TOK)).T
     keep = keep_s[pl.ds(pl.multiple_of(pl.program_id(0) * count, count), count), :] > 0.0
@@ -110,13 +113,14 @@
     angle = angles(by_frame, within, s)
     for k in range(GROUPS):
         for i, h in enumerate(heads):
-            head = k * LOCAL_HEADS + h
-            at = slice(head * HEAD_DIM, (head + 1) * HEAD_DIM)
+            head = (k if ups is None else jnp.bitwise_xor(s, k)) * LOCAL_HEADS + h
+            at = pl.ds(pl.multiple_of(head * HEAD_DIM, HEAD_DIM), HEAD_DIM)
+            out = outs.at[k] if ups is None else outs[k]
             for n, (raw, gain) in enumerate(((query, gain_q), (key, gain_k))):
-                normed = raw[:, at].astype(F32) * rhos[n] * gain[head : head + 1, :]
-                outs[k, 4 * i + n] = turn(normed, angle, 1).astype(BF)
-            outs[k, 4 * i + 2] = value[:, at]
-            outs[k, 4 * i + 3] = jnp.where(keep, cot[:, at].astype(F32), 0.0).astype(BF)
+                normed = raw[:, at].astype(F32) * rhos[n] * gain[pl.ds(head, 1), :]
+                out[4 * i + n] = turn(normed, angle, 1).astype(BF)
+            out[4 * i + 2] = value[:, at]
+            out[4 * i + 3] = jnp.where(keep, cot[:, at].astype(F32), 0.0).astype(BF)
     if ups is None:
         return
     rows = []
@@ -139,37 +143,46 @@
         extra = jnp.where(at_row == 2 * n + 1, wide - high, extra)
     aux = jnp.concatenate([down, extra], 0).astype(BF)
     for k in range(GROUPS):
-        outs[k, 4] = aux
-
-
-def attend_kernel(base, last, flags, packs, gain_q, gain_k, by_frame, *refs):
+        outs[k][4] = aux
+
+
+def attend_kernel(base, flags, *refs):
+    last = base == LOCAL_HEADS - 1
+    s = lax.axis_index("seq")
     if last:
-        state, refs = refs[0], refs[1:]
+        packs, refs = refs[:GROUPS], refs[GROUPS:]
+        frames = [jnp.bitwise_xor(s, k) for k in range(GROUPS)]
+    else:
+        packs, refs = [refs[0].at[k] for k in range(GROUPS)], refs[1:]
+        frames = list(range(GROUPS))
+    gain_q, gain_k, by_frame, *refs = refs
+    if base == 0:
+        within, ups_all, *refs = refs
+    else:
+        state, *refs = refs
         before = state
+        if last:
+            before, *refs = refs
         within = [state[HELD + n * FRAME_TOK : HELD + (n + 1) * FRAME_TOK, :] for n in range(3)]
-        first = HELD + 3 * FRAME_TOK
+        first = HELD + 3 * FRAME_TOK + (base - 1) * 96
         ups = [state[first + n * RANK : first + (n + 1) * RANK, :].astype(BF) for n in range(3)]
-    else:
-        within, ups_all, *refs = refs
     wide_out, summed = refs[:2]
     refs = refs[2:]
     if last:
         mean_out, *mix = refs[:4]
         refs = refs[4:]
     q_s, k_s, kt_s, v_s, g_s, sc, dp, pb, db, dk_acc, dv_acc, dq_s, prod_s, sums = refs
-    s = lax.axis_index("seq")
-    step = pl.program_id(0)
-    head = s * LOCAL_HEADS + base + step
+    head = s * LOCAL_HEADS + base
     owner = []
     for k in range(GROUPS):
-        owner.append(flags[0, k] + (owner[-1] if k else 0))
+        owner.append(sum(jnp.where(f <= frames[k], flags[0, f], 0) for f in range(FRAMES)))
         at = slice(k * FRAME_TOK, (k + 1) * FRAME_TOK)
-        q_s[at, :] = packs[k, 0]
-        key = packs[k, 1]
+        q_s[at, :] = packs[k][0]
+        key = packs[k][1]
         k_s[at, :] = key
         kt_s[:, at] = key.astype(F32).T.astype(BF)
-        v_s[at, :] = packs[k, 2]
-        g_s[at, :] = packs[k, 3]
+        v_s[at, :] = packs[k][2]
+        g_s[at, :] = packs[k][3]
     factor = SCALING * math.log2(math.e)
     lane = lax.broadcasted_iota(jnp.int32, (1, 256), 1)
     for t in range(4):
@@ -208,13 +221,13 @@
             dv_acc[...] += dv
             dk_acc[...] += dk
         dq_s[tile, :] = nn(kt_s[...], db[b]).T
-    if not last:
+    if base == 0:
         up_at = pl.ds(pl.multiple_of(head * HEAD_DIM, HEAD_DIM), HEAD_DIM)
         ups = [ups_all[n, :, up_at] for n in range(3)]
     gains = [gain[pl.ds(head, 1), :] for gain in (gain_q, gain_k)]
     for k in range(GROUPS):
         at = slice(k * FRAME_TOK, (k + 1) * FRAME_TOK)
-        angle = angles(by_frame, within, k)
+        angle = angles(by_frame, within, frames[k])
         for n, (acc, rot) in enumerate(((dq_s, q_s), (dk_acc, k_s))):
             grad = (acc[at, :] * SCALING).astype(BF).astype(F32)
             wide = gains[n] * turn(grad, angle, -1)
@@ -229,29 +242,33 @@
         part = full[:, k * FRAME_TOK : (k + 1) * FRAME_TOK]
         at = slice(k * 112, (k + 1) * 112)
         if last:
+            at = pl.ds(pl.multiple_of(frames[k] * 112, 8), 112)
             sums[k] = part + before[at, :]
+        elif base == 0:
+            summed[at, :] = part
         else:
-            summed[at, :] = part + jnp.where(step > 0, summed[at, :], 0.0)
-    if not last:
-        later = pl.ds(pl.multiple_of((s * LOCAL_HEADS + 2) * HEAD_DIM, HEAD_DIM), HEAD_DIM)
+            summed[at, :] = part + before[at, :]
+    if base == 0:
         for n in range(3):
             summed[HELD + n * FRAME_TOK : HELD + (n + 1) * FRAME_TOK, :] = within[n]
-            first = HELD + 3 * FRAME_TOK + n * RANK
-            summed[first : first + RANK, :] = ups_all[n, :, later].astype(F32)
+            for h in range(1, LOCAL_HEADS):
+                at = pl.ds(pl.multiple_of((head + h) * HEAD_DIM, HEAD_DIM), HEAD_DIM)
+                first = HELD + 3 * FRAME_TOK + (h - 1) * 96 + n * RANK
+                summed[first : first + RANK, :] = ups_all[n, :, at].astype(F32)
+    if not last:
         return
     at_row = lax.broadcasted_iota(jnp.int32, (8, FRAME_TOK), 0)
     for n in range(2):
         gathered = jnp.zeros((8, FRAME_TOK), F32)
         for k in range(GROUPS):
-            row = sums[jnp.bitwise_xor(s, k), 96 + 8 * n : 104 + 8 * n]
+            row = sums[k, 96 + 8 * n : 104 + 8 * n]
             gathered = jnp.where(at_row == k, row, gathered)
         mean_out[8 * n : 8 * n + 8, :] = gathered
     tail = halves(mean_out[...])
     for b in range(2):
-        summed[b] = sums[jnp.bitwise_xor(s, b), 0:96]
+        summed[b] = sums[b, 0:96]
         for a in range(1, 4):
-            away = jnp.bitwise_xor(s, 2 * a + b)
-            mix[a - 1][b * 96 : (b + 1) * 96, :] = sums[away, 0:96].astype(BF)
+            mix[a - 1][b * 96 : (b + 1) * 96, :] = sums[2 * a + b, 0:96].astype(BF)
     for a in range(1, 4):
         mix[a - 1][192:224, :] = tail
 
@@ -310,42 +327,48 @@
                     send[b, k] = part.astype(BF)
 
 
-def up_kernel(means, firsts, lasts, wide01, wide2, *refs):
-    gain_q, gain_k, by_frame, within, keep, send, turned_s, up_s = refs
-    wides = [wide01.at[0], wide01.at[1], wide2.at[0]]
+def up_kernel(means, firsts, *refs):
+    lasts, wides = refs[:GROUPS], [ref.at[0] for ref in refs[GROUPS : GROUPS + 3]]
+    gain_q, gain_k, by_frame, within, keep, send, turned_s, up_s, scaled_s = refs[GROUPS + 3 :]
     s, _, x, c = position()
     xl = jnp.bitwise_and(x, 1)
-    for h in range(LOCAL_HEADS):
-        lanes = slice(h * HEAD_DIM, (h + 1) * HEAD_DIM)
-        for k in range(GROUPS):
-            at = slice(k * FRAME_TOK, (k + 1) * FRAME_TOK)
-            angle = angles(by_frame, within, k)
+    order = [jnp.bitwise_xor(s, k) for k in range(GROUPS)]
+    for k in range(GROUPS):
+        at = slice(k * FRAME_TOK, (k + 1) * FRAME_TOK)
+        for h in range(LOCAL_HEADS):
+            lanes = slice(h * HEAD_DIM, (h + 1) * HEAD_DIM)
+            if h != 1:
+                angle = angles(by_frame, within, order[k] if h == 2 else k)
             for n in range(2):
-                rot = (lasts if h == 2 else firsts)[k, 4 * (h % 2) + n].astype(F32)
-                turned_s[n, at, lanes] = turn(rot, angle, -1).astype(BF)
-    for n in range(3):
-        plain_hi, plain_lo, along = [], [], []
-        for p in range(GROUPS):
-            aux = lasts[p, 4].astype(F32)
+                rot = lasts[k][n] if h == 2 else firsts[k, 4 * h + n]
+                turned_s[n, at, lanes] = turn(rot.astype(F32), angle, -1).astype(BF)
+    for p in range(GROUPS):
+        aux = lasts[p][4].astype(F32)
+        for n in range(3):
             down = aux[n * RANK : (n + 1) * RANK]
             if n == 2:
-                plain_hi.append(down.astype(BF))
+                scaled_s[p, n, 0] = down.astype(BF)
                 continue
             rho = aux[96 + 2 * n : 97 + 2 * n] + aux[97 + 2 * n : 98 + 2 * n]
-            mean = means[pl.ds(8 * n + jnp.bitwise_xor(s, p), 1), :]
             scaled = down * rho
             high = scaled.astype(BF)
-            plain_hi.append(high)
-            plain_lo.append((scaled - high.astype(F32)).astype(BF))
-            along.append((scaled * (mean * (1.0 / CHANNELS))).astype(BF))
-        high = jnp.concatenate(plain_hi, 1)
+            mean = means[8 * n + p : 8 * n + p + 1, :] * (1.0 / CHANNELS)
+            scaled_s[p, n, 0] = high
+            scaled_s[p, n, 1] = (scaled - high.astype(F32)).astype(BF)
+            scaled_s[p, n, 2] = (scaled * mean).astype(BF)
+
+    def rows(n, kind, h):
+        places = range(GROUPS) if h == 2 else order
+        return jnp.concatenate([scaled_s[p, n, kind] for p in places], 1)
+
+    for n in range(3):
         for h in range(LOCAL_HEADS):
             lanes = slice(h * HEAD_DIM, (h + 1) * HEAD_DIM)
-            out = nn(high, wides[h][n])
+            out = nn(rows(n, 0, h), wides[h][n])
             if n < 2:
                 gain = (gain_q, gain_k)[n][pl.ds(s * LOCAL_HEADS + h, 1), :]
-                out = out + nn(jnp.concatenate(plain_lo, 1), wides[h][n])
-                out = out - nn(jnp.concatenate(along, 1), turned_s[n, :, lanes]) / gain
+                out = out + nn(rows(n, 1, h), wides[h][n])
+                out = out - nn(rows(n, 2, h), turned_s[n, :, lanes]) / gain
             up_s[n * RANK : (n + 1) * RANK, lanes] = out
     for a in range(2):
         for b in range(2):
@@ -468,39 +491,38 @@
     count = FRAME_TOK // steps
     specs = [pl.BlockSpec((count, CHANNELS), lambda i: (i, 0))] * 4 + [whole(a) for a in ins[4:]]
     specs[8] = pl.BlockSpec((3, count, HEAD_DIM), lambda i: (0, i, 0))
-    slots = outs[0].shape[1]
-    out_specs = [pl.BlockSpec((GROUPS, slots, count, HEAD_DIM), lambda i: (0, 0, i, 0))]
+    out_specs = [whole(a) for a in outs]
+    if len(outs) == 1:
+        out_specs = [pl.BlockSpec((GROUPS, 8, count, HEAD_DIM), lambda i: (0, 0, i, 0))]
     return pl.pallas_call(
         functools.partial(pack_kernel, heads),
         grid=(steps,),
         out_shape=outs,
         in_specs=specs,
-        out_specs=out_specs + [whole(a) for a in outs[1:]],
+        out_specs=out_specs,
         scratch_shapes=[pltpu.VMEM((FRAME_TOK, FRAME_TOK), F32)],
         compiler_params=params(BIG),
     )(*ins)
 
 
-def attend(base, heads, ins, before):
-    last = before is not None
+def attend(base, ins):
     seq_len = FRAMES * FRAME_TOK
     rows = (seq_len, HEAD_DIM)
-    piece = pl.BlockSpec((GROUPS, 4, FRAME_TOK, HEAD_DIM), lambda i: (0, i, 0, 0))
-    specs = [SMEM, piece] + [whole(a) for a in ins[2:]]
-    outs = [shape((heads, 3, *rows))]
-    out_specs = [pl.BlockSpec((1, 3, *rows), lambda i: (i, 0, 0, 0))]
-    if last:
-        ins = [*ins, before]
-        specs.append(whole(before))
+    outs = [shape((1, 3, *rows))]
+    out_specs = [whole(outs[0])]
+    if base == LOCAL_HEADS - 1:
+        specs = [SMEM] + [pl.BlockSpec((4, FRAME_TOK, HEAD_DIM), lambda i: (0, 0, 0))] * GROUPS
         extra = [shape((2, 96, FRAME_TOK), F32), shape((16, FRAME_TOK), F32)]
         extra += [shape((224, FRAME_TOK))] * 3
         out_specs += [VMEM] * 5
     else:
-        extra = [shape((HELD + 3 * FRAME_TOK + 96, FRAME_TOK), F32)]
+        specs = [SMEM, pl.BlockSpec((GROUPS, 4, FRAME_TOK, HEAD_DIM), lambda i: (0, base, 0, 0))]
+        extra = [shape((HELD + (1 - base) * (3 * FRAME_TOK + 192), FRAME_TOK), F32)]
         out_specs += [whole(a) for a in extra]
+    specs += [whole(a) for a in ins[len(specs) :]]
     return pl.pallas_call(
-        functools.partial(attend_kernel, base, last),
-        grid=(heads,),
+        functools.partial(attend_kernel, base),
+        grid=(1,),
         out_shape=outs + extra,
         in_specs=specs,
         out_specs=out_specs,
@@ -522,9 +544,9 @@
         ],
         compiler_params=params(32),
         cost_estimate=pl.CostEstimate(
-            flops=10 * heads * seq_len * seq_len * HEAD_DIM,
-            bytes_accessed=heads * (4 << 20),
-            transcendentals=heads * seq_len * seq_len,
+            flops=10 * seq_len * seq_len * HEAD_DIM,
+            bytes_accessed=4 << 20,
+            transcendentals=seq_len * seq_len,
         ),
     )(*ins)
 
@@ -552,16 +574,20 @@
     raws = [query_unnormed[0], key_unnormed[0], value_projected[0], cotangent[0]]
     first = [*raws, generated_mask[0], *norms]
     (firsts,) = pack(first, (0, 1), [shape((GROUPS, 8, FRAME_TOK, HEAD_DIM))], 4)
-    lasts, local = pack(
+    *lasts, local = pack(
         first + [adapter_up_maps, downs, tokens],
         (2,),
-        [shape((GROUPS, 5, FRAME_TOK, HEAD_DIM)), shape((80, FRAME_TOK), F32)],
+        [shape((5, FRAME_TOK, HEAD_DIM))] * GROUPS + [shape((80, FRAME_TOK), F32)],
         1,
     )
     firsts = lax.all_to_all(firsts, "seq", 0, 0, tiled=True)
-    lasts = lax.all_to_all(lasts, "seq", 0, 0, tiled=True)
-    wide01, before = attend(0, 2, [block_begin_flags, firsts, *norms, adapter_up_maps], None)
-    wide2, kept, means, *mix = attend(2, 1, [block_begin_flags, lasts, *norms[:3]], before)
+    wide0, state = attend(0, [block_begin_flags, firsts, *norms, adapter_up_maps])
+    state, lasts[2], lasts[6] = lax.optimization_barrier((state, lasts[2], lasts[6]))
+    lasts = lasts[:1] + [seq_swap(lasts[k], k) for k in range(1, GROUPS)]
+    wide1, summed = attend(1, [block_begin_flags, firsts, *norms[:3], state])
+    wide2, kept, means, *mix = attend(
+        2, [block_begin_flags, *lasts, *norms[:3], state, summed]
+    )
     mix = [swap(mix[a - 1], dy=a) for a in range(1, 4)]
     kept, means, mix = call(
         mix_kernel,
@@ -578,9 +604,13 @@
     )
     up_keep, up_send = call(
         up_kernel,
-        [means, firsts, lasts, wide01, wide2, *norms],
+        [means, firsts, *lasts, wide0, wide1, wide2, *norms],
         [shape((2, 24, GCOLS), F32), shape((2, 24, GCOLS))],
-        [pltpu.VMEM((2, 1024, GCOLS), BF), pltpu.VMEM((96, GCOLS), F32)],
+        [
+            pltpu.VMEM((2, 1024, GCOLS), BF),
+            pltpu.VMEM((96, GCOLS), F32),
+            pltpu.VMEM((GROUPS, 3, 3, RANK, FRAME_TOK), BF),
+        ],
         mib=24,
     )
     got = swap(send, dc=1)

time: 145 us -> 140 us (0.966)
  waiting for transfers between devices: 51.6 us -> 45.4 us
  local copies, waits for them, and re-layouts: 5.16 us -> 1.45 us
  starting transfers between devices: 55.9 us -> 59.2 us
  Pallas kernels: 31.2 us -> 33 us
    all_to_all x1, waiting for transfers between devices: 21.9 us -> 11.1 us  [shards(): firsts = lax.all_to_all(firsts, 'seq', 0, 0, tiled=True)]
    ppermute x24 -> x31, waiting for transfers between devices: 26.3 us -> 34.3 us  [swap(): return lax.ppermute(array, ('seq', 'dp'), pairs)]
    ppermute x24 -> x31, starting transfers between devices: 44.6 us -> 51.7 us  [swap(): return lax.ppermute(array, ('seq', 'dp'), pairs)]
    all_to_all x1 -> x0, starting transfers between devices: 3.83 us -> none  [shards(): lasts = lax.all_to_all(lasts, 'seq', 0, 0, tiled=True)]
    unnamed x26 -> x24, local copies, waits for them, and re-layouts: 5.16 us -> 1.45 us
    all_to_all x1 -> x0, waiting for transfers between devices: 3.35 us -> none  [shards(): lasts = lax.all_to_all(lasts, 'seq', 0, 0, tiled=True)]
    pallas_call x2 -> x3, Pallas kernels: 16.4 us -> 17.3 us  [attend(): pl.pallas_call(functools.partial(attend_kernel, base), grid=(1,), out_sha...]
  transfers between devices with their start and end apart: 26 -> 32, of which waited for: 19 -> 19; matrix products, arithmetic and copies ran while one was open for 0% -> 0% of each run, Pallas kernels for 13% -> 14%
where the time goes in v2:
time: 140 us
  starting transfers between devices  59.2 us (42%)
  waiting for transfers between devices  45.4 us (32%)
  Pallas kernels  33 us (24%)
  local copies, waits for them, and re-layouts  1.45 us (1%)
    ppermute x31, starting transfers between devices, swap(): return lax.ppermute(array, ('seq', 'dp'), pairs)  51.7 us
    ppermute x31, waiting for transfers between devices, swap(): return lax.ppermute(array, ('seq', 'dp'), pairs)  34.3 us
    pallas_call x3, Pallas kernels, attend(): pl.pallas_call(functools.partial(attend_kernel, base), grid=(1,), out_sha...  17.3 us
    all_to_all x1, waiting for transfers between devices, shards(): firsts = lax.all_to_all(firsts, 'seq', 0, 0, tiled=True)  11.1 us
    pallas_call x2, Pallas kernels, pack(): pl.pallas_call(functools.partial(pack_kernel, heads), grid=(steps,), out_...  10.9 us
    all_to_all x1, starting transfers between devices, shards(): firsts = lax.all_to_all(firsts, 'seq', 0, 0, tiled=True)  7.48 us
    pallas_call x12, Pallas kernels, call(): pl.pallas_call(kernel, out_shape=outs, in_specs=[SMEM] * smem + [VMEM] *...  4.9 us
  transfers between devices with their start and end apart: 32, of which 19 were waited for; matrix products, arithmetic and copies ran while one was open for 0% of the time, Pallas kernels for 14%

profile of v2, /device:TPU:1, one launch (start us, length us, event | category | flops | bytes accessed | tf_op | source)
XLA Modules:
  0.0 139.9 jit_solution(4135785783304901445)
XLA Ops:
  0.6 5.2 %shard_map.141 = bf16[8,8,128,128]{3,2,1,0:T(8,128)(2,1)} custom-call(bf16[128,3072]{1,0:T(8,128)(2,1)} %bitcast.25, bf16[128,3072]{1,0:T(8,128)(2,1)} %bitcast.27, bf16[128,3072]{1,0:T(8,128)(2,1)} %bitcast.29, bf16[128,3072]{1,0:T(8,128)(2,1)} %bitcast.31, s32[1,128]{1,0:T(1,128)} %bitcast.34, f32[24,128]{1,0:T(8,128)} %bitcast.13, f32[24,128]{1,0:T(8,128)} %bitcast.19, ...), custom_call_target="tpu_custom_call" | custom-call | tf_op jit(solution)/shard_map/pallas_call | solution.py:497
  5.8 7.5 %all-to-all-start = ((bf16[8,8,128,128]{3,2,1,0:T(8,128)(2,1)}), bf16[8,8,128,128]{3,2,1,0:T(8,128)(2,1)S(1)}, u32[]{:S(2)}, u32[]{:S(2)}) async-start(bf16[8,8,128,128]{3,2,1,0:T(8,128)(2,1)} %shard_map.141), calls=%async_computation | async-start | bytes 4194304 | tf_op jit(solution)/shard_map/all_to_all | solution.py:583
  13.4 5.7 %shard_map.140 = (bf16[5,128,128]{2,1,0:T(8,128)(2,1)}, bf16[5,128,128]{2,1,0:T(8,128)(2,1)}, bf16[5,128,128]{2,1,0:T(8,128)(2,1)}, bf16[5,128,128]{2,1,0:T(8,12...) custom-call(bf16[128,3072]{1,0:T(8,128)(2,1)} %bitcast.26, ...), custom_call_target="tpu_custom_call" | custom-call | tf_op jit(solution)/shard_map/pallas_call | solution.py:497
  19.0 3.0 %collective-permute-start = (bf16[5,128,128]{2,1,0:T(8,128)(2,1)}, bf16[5,128,128]{2,1,0:T(8,128)(2,1)S(1)}, u32[]{:S(2)}, u32[]{:S(2)}) collective-permute-start(bf16[5,128,128]{2,1,0:T(8,128)(2,1)} %get-tuple-element.45), channel_id=1, source_target_pairs={{0,32},{1,33},{4,36},{5,37},{8,40},{9,41},{12,44},{13,45},{16,48},... | collective-permute-start | bytes 491528 | tf_op jit(solution)/shard_map/ppermute | solution.py:478
  22.1 1.2 collective-permute-start.2
  23.2 2.4 %collective-permute-start.3 = (bf16[5,128,128]{2,1,0:T(8,128)(2,1)}, bf16[5,128,128]{2,1,0:T(8,128)(2,1)S(1)}, u32[]{:S(2)}, u32[]{:S(2)}) collective-permute-start(bf16[5,128,128]{2,1,0:T(8,128)(2,1)} %get-tuple-element.51), channel_id=1, source_target_pairs={{0,128},{1,129},{4,132},{5,133},{8,136},{9,137},{12,140},{13,141},... | collective-permute-start | bytes 491528 | tf_op jit(solution)/shard_map/ppermute | solution.py:478
  25.6 3.0 %collective-permute-start.4 = (bf16[5,128,128]{2,1,0:T(8,128)(2,1)}, bf16[5,128,128]{2,1,0:T(8,128)(2,1)S(1)}, u32[]{:S(2)}, u32[]{:S(2)}) collective-permute-start(bf16[5,128,128]{2,1,0:T(8,128)(2,1)} %get-tuple-element.52), channel_id=1, source_target_pairs={{0,160},{1,161},{4,164},{5,165},{8,168},{9,169},{12,172},{13,173},... | collective-permute-start | bytes 491528 | tf_op jit(solution)/shard_map/ppermute | solution.py:478
  28.6 1.8 %collective-permute-start.6 = (bf16[5,128,128]{2,1,0:T(8,128)(2,1)}, bf16[5,128,128]{2,1,0:T(8,128)(2,1)}, u32[]{:S(2)}, u32[]{:S(2)}) collective-permute-start(bf16[5,128,128]{2,1,0:T(8,128)(2,1)} %get-tuple-element.54), channel_id=1, source_target_pairs={{0,224},{1,225},{4,228},{5,229},{8,232},{9,233},{12,236},{13,237},... | collective-permute-start | bytes 491528 | tf_op jit(solution)/shard_map/ppermute | solution.py:478
  30.4 11.1 %all-to-all-done.refs_0_.firsts = bf16[8,8,128,128]{3,2,1,0:T(8,128)(2,1)S(1)} async-done(((bf16[8,8,128,128]{3,2,1,0:T(8,128)(2,1)}), bf16[8,8,128,128]{3,2,1,0:T(8,128)(2,1)S(1)}, u32[]{:S(2)}, u32[]{:S(2)}) %all-to-all-start) | async-done | bytes 2097184 | tf_op jit(solution)/shard_map/all_to_all | solution.py:583
  41.6 0.7 copy-done.5
  42.3 0.7 copy-done.6
  43.0 5.6 %shard_map.142 = (bf16[1,3,1024,128]{3,2,1,0:T(8,128)(2,1)S(1)}, f32[1472,128]{1,0:T(8,128)S(1)}) custom-call(s32[1,8]{1,0:T(1,128)S(1)} %copy-done.9, bf16[8,8,128,128]{3,2,1,0:T(8,128)(2,1)S(1)} %all-to-all-done.refs_0_.firsts, f32[24,128]{1,0:T(8,128)S(1)} %bitcast.15, f32[24,128]{1,0:T(8,128)S(1)} %bitcast.21, f32[24,128]{1,0:T(8,128)S(1)} %copy-done.6, ...), custom_call_target="tpu_custom_call" | custom-call | flops 1342177280 | bytes 4194304 | tf_op jit(solution)/shard_map/pallas_call | solution.py:523
  48.7 0.7 collective-permute-start.5
  49.5 5.6 %shard_map.143 = (bf16[1,3,1024,128]{3,2,1,0:T(8,128)(2,1)S(1)}, f32[896,128]{1,0:T(8,128)S(1)}) custom-call(s32[1,8]{1,0:T(1,128)S(1)} %copy-done.9, bf16[8,8,128,128]{3,2,1,0:T(8,128)(2,1)S(1)} %all-to-all-done.refs_0_.firsts, f32[24,128]{1,0:T(8,128)S(1)} %bitcast.16, f32[24,128]{1,0:T(8,128)S(1)} %bitcast.22, f32[24,128]{1,0:T(8,128)S(1)} %copy-done.6, ...), custom_call_target="tpu_custom_call" | custom-call | flops 1342177280 | bytes 4194304 | tf_op jit(solution)/shard_map/pallas_call | solution.py:523
  55.1 0.7 collective-permute-done.6.refs_7_
  55.8 5.0 %collective-permute-done.5.refs_6_ = bf16[5,128,128]{2,1,0:T(8,128)(2,1)S(1)} collective-permute-done((bf16[5,128,128]{2,1,0:T(8,128)(2,1)S(1)}, bf16[5,128,128]{2,1,0:T(8,128)(2,1)S(1)}, u32[]{:S(2)}, u32[]{:S(2)}) %collective-permute-start.5) | collective-permute-done | bytes 163872 | tf_op jit(solution)/shard_map/ppermute | solution.py:478
  60.8 6.1 %shard_map.144 = (bf16[1,3,1024,128]{3,2,1,0:T(8,128)(2,1)S(1)}, f32[2,96,128]{2,1,0:T(8,128)S(1)}, f32[16,128]{1,0:T(8,128)S(1)}, bf16[224,128]{1,0:T(8,128)(2,...) custom-call(s32[1,8]{1,0:T(1,128)S(1)} %copy-done.9, bf16[5,128,128]{2,1,0:T(8,128)(2,1)S(1)} %copy-done.3, ...), custom_call_target="tpu_custom_call" | custom-call | flops 1342177280 | bytes 4194304 | tf_op jit(solution)/shard_map/pallas_call | solution.py:523
  67.2 1.7 %collective-permute-start.8 = (bf16[224,128]{1,0:T(8,128)(2,1)S(1)}, bf16[224,128]{1,0:T(8,128)(2,1)S(1)}, u32[]{:S(2)}, u32[]{:S(2)}) collective-permute-start(bf16[224,128]{1,0:T(8,128)(2,1)S(1)} %get-tuple-element.60), channel_id=1, source_target_pairs={{0,128},{1,129},{4,132},{5,133},{8,136},{9,137},{12,140},{13,141},... | collective-permute-start | bytes 172040 | tf_op jit(solution)/shard_map/ppermute | solution.py:478
  68.9 1.9 %collective-permute-start.9 = (bf16[224,128]{1,0:T(8,128)(2,1)S(1)}, bf16[224,128]{1,0:T(8,128)(2,1)S(1)}, u32[]{:S(2)}, u32[]{:S(2)}) collective-permute-start(bf16[224,128]{1,0:T(8,128)(2,1)S(1)} %get-tuple-element.61), channel_id=1, source_target_pairs={{0,192},{1,193},{4,196},{5,197},{8,200},{9,201},{12,204},{13,205},... | collective-permute-start | bytes 172040 | tf_op jit(solution)/shard_map/ppermute | solution.py:478
  70.8 1.2 collective-permute-done.8.r2
  72.0 1.6 %collective-permute-done.9.r3 = bf16[224,128]{1,0:T(8,128)(2,1)S(1)} collective-permute-done((bf16[224,128]{1,0:T(8,128)(2,1)S(1)}, bf16[224,128]{1,0:T(8,128)(2,1)S(1)}, u32[]{:S(2)}, u32[]{:S(2)}) %collective-permute-start.9) | collective-permute-done | bytes 57376 | tf_op jit(solution)/shard_map/ppermute | solution.py:478
  73.7 4.3 %collective-permute-done.10.got = bf16[128,128]{1,0:T(8,128)(2,1)S(1)} collective-permute-done((bf16[128,128]{1,0:T(8,128)(2,1)S(1)}, bf16[128,128]{1,0:T(8,128)(2,1)S(1)}, u32[]{:S(2)}, u32[]{:S(2)}) %collective-permute-start.10) | collective-permute-done | bytes 32800 | tf_op jit(solution)/shard_map/ppermute | solution.py:478
  78.4 3.2 %collective-permute-start.11 = (bf16[4,4,24,640]{3,2,1,0:T(8,128)(2,1)S(1)}, bf16[4,4,24,640]{3,2,1,0:T(8,128)(2,1)S(1)}, u32[]{:S(2)}, u32[]{:S(2)}) collective-permute-start(bf16[4,4,24,640]{3,2,1,0:T(8,128)(2,1)S(1)} %get-tuple-element.67), channel_id=1, source_target_pairs={{0,1},{1,0},{4,5},{5,4},{8,9},{9,8},{12,13},{13,12},{16,17},{17,16... | collective-permute-start | bytes 1474568 | tf_op jit(solution)/shard_map/ppermute | solution.py:478
  81.6 1.5 %collective-permute-done.11.got = bf16[4,4,24,640]{3,2,1,0:T(8,128)(2,1)S(1)} collective-permute-done((bf16[4,4,24,640]{3,2,1,0:T(8,128)(2,1)S(1)}, bf16[4,4,24,640]{3,2,1,0:T(8,128)(2,1)S(1)}, u32[]{:S(2)}, u32[]{:S(2)}) %collective-permute-start.11) | collective-permute-done | bytes 491552 | tf_op jit(solution)/shard_map/ppermute | solution.py:478
  83.2 0.6 collective-permute-start.12
  84.2 3.0 %collective-permute-start.14 = (bf16[4,24,640]{2,1,0:T(8,128)(2,1)S(1)}, bf16[4,24,640]{2,1,0:T(8,128)(2,1)S(1)}, u32[]{:S(2)}, u32[]{:S(2)}) collective-permute-start(bf16[4,24,640]{2,1,0:T(8,128)(2,1)S(1)} %get-tuple-element.71), channel_id=1, source_target_pairs={{0,34},{1,35},{4,38},{5,39},{8,42},{9,43},{12,46},{13,47},{16,50},... | collective-permute-start | bytes 368648 | tf_op jit(solution)/shard_map/ppermute | solution.py:478
  87.2 2.7 %shard_map.149 = (f32[2,24,384]{2,1,0:T(8,128)S(1)}, bf16[2,24,384]{2,1,0:T(8,128)(2,1)S(1)}) custom-call(f32[16,128]{1,0:T(8,128)S(1)} %get-tuple-element.76.means, bf16[8,8,128,128]{3,2,1,0:T(8,128)(2,1)S(1)} %all-to-all-done.refs_0_.firsts, bf16[5,128,128]{2,1,0:T(8,128)(2,1)S(1)} %copy-done.3, bf16[5,128,128]{2,1,0:T(8,128)(2,1)S(1)} %collective-permute-done.refs_1_, ...), custom_call_target="tpu_custom_call" | custom-call | tf_op jit(solution)/shard_map/pallas_call | solution.py:456
  89.9 1.3 collective-permute-start.18
  91.2 2.0 %collective-permute-done.14.r3 = bf16[4,24,640]{2,1,0:T(8,128)(2,1)S(1)} collective-permute-done((bf16[4,24,640]{2,1,0:T(8,128)(2,1)S(1)}, bf16[4,24,640]{2,1,0:T(8,128)(2,1)S(1)}, u32[]{:S(2)}, u32[]{:S(2)}) %collective-permute-start.14) | collective-permute-done | bytes 122912 | tf_op jit(solution)/shard_map/ppermute | solution.py:478
  93.4 3.0 %collective-permute-start.16 = (bf16[24,640]{1,0:T(8,128)(2,1)S(1)}, bf16[24,640]{1,0:T(8,128)(2,1)S(1)}, u32[]{:S(2)}, u32[]{:S(2)}) collective-permute-start(bf16[24,640]{1,0:T(8,128)(2,1)S(1)} %get-tuple-element.74), channel_id=1, source_target_pairs={{0,128},{1,129},{4,132},{5,133},{8,136},{9,137},{12,140},{13,141},... | collective-permute-start | bytes 92168 | tf_op jit(solution)/shard_map/ppermute | solution.py:478
  96.3 0.9 collective-permute-start.17
  97.3 2.6 %collective-permute-done.19.up_got = bf16[24,384]{1,0:T(8,128)(2,1)S(1)} collective-permute-done((bf16[24,384]{1,0:T(8,128)(2,1)S(1)}, bf16[24,384]{1,0:T(8,128)(2,1)S(1)}, u32[]{:S(2)}, u32[]{:S(2)}) %collective-permute-start.19) | collective-permute-done | bytes 18464 | tf_op jit(solution)/shard_map/ppermute | solution.py:478
  100.3 4.4 %collective-permute-start.22 = (bf16[24,1024]{1,0:T(8,128)(2,1)S(1)}, bf16[24,1024]{1,0:T(8,128)(2,1)S(1)}, u32[]{:S(2)}, u32[]{:S(2)}) collective-permute-start(bf16[24,1024]{1,0:T(8,128)(2,1)S(1)} %shard_map.151.own), channel_id=1, source_target_pairs={{0,12},{1,13},{4,8},{5,9},{8,4},{9,5},{12,0},{13,1},{16,28},{17,29... | collective-permute-start | bytes 147464 | tf_op jit(solution)/shard_map/ppermute | solution.py:478
  105.1 1.1 collective-permute-done.22.r3
  106.2 2.9 %collective-permute-done.21.r2 = bf16[24,1024]{1,0:T(8,128)(2,1)S(1)} collective-permute-done((bf16[24,1024]{1,0:T(8,128)(2,1)S(1)}, bf16[24,1024]{1,0:T(8,128)(2,1)S(1)}, u32[]{:S(2)}, u32[]{:S(2)}) %collective-permute-start.21) | collective-permute-done | bytes 49184 | tf_op jit(solution)/shard_map/ppermute | solution.py:478
  109.2 3.0 %collective-permute-start.23 = (bf16[24,1024]{1,0:T(8,128)(2,1)S(1)}, bf16[24,1024]{1,0:T(8,128)(2,1)S(1)}, u32[]{:S(2)}, u32[]{:S(2)}) collective-permute-start(bf16[24,1024]{1,0:T(8,128)(2,1)S(1)} %shard_map.152.own), channel_id=1, source_target_pairs={{0,28},{1,29},{4,24},{5,25},{8,20},{9,21},{12,16},{13,17},{16,12},... | collective-permute-start | bytes 147464 | tf_op jit(solution)/shard_map/ppermute | solution.py:478
  112.2 1.5 %collective-permute-done.23.got = bf16[24,1024]{1,0:T(8,128)(2,1)S(1)} collective-permute-done((bf16[24,1024]{1,0:T(8,128)(2,1)S(1)}, bf16[24,1024]{1,0:T(8,128)(2,1)S(1)}, u32[]{:S(2)}, u32[]{:S(2)}) %collective-permute-start.23) | collective-permute-done | bytes 49184 | tf_op jit(solution)/shard_map/ppermute | solution.py:478
  113.7 1.3 collective-permute-start.26
  115.0 2.0 %collective-permute-start.24 = (bf16[24,1024]{1,0:T(8,128)(2,1)S(1)}, bf16[24,1024]{1,0:T(8,128)(2,1)S(1)}, u32[]{:S(2)}, u32[]{:S(2)}) collective-permute-start(bf16[24,1024]{1,0:T(8,128)(2,1)S(1)} %shard_map.153.refs_0_), channel_id=1, source_target_pairs={{0,64},{1,65},{4,68},{5,69},{8,72},{9,73},{12,76},{13,77},{16,80},... | collective-permute-start | bytes 147464 | tf_op jit(solution)/shard_map/ppermute | solution.py:478
  117.1 0.9 collective-permute-done.26.refs_3_
  118.0 1.5 %collective-permute-done.25.refs_2_ = bf16[24,1024]{1,0:T(8,128)(2,1)S(1)} collective-permute-done((bf16[24,1024]{1,0:T(8,128)(2,1)S(1)}, bf16[24,1024]{1,0:T(8,128)(2,1)S(1)}, u32[]{:S(2)}, u32[]{:S(2)}) %collective-permute-start.25) | collective-permute-done | bytes 49184 | tf_op jit(solution)/shard_map/ppermute | solution.py:478
  119.5 2.4 %collective-permute-start.29 = (bf16[4,24,1024]{2,1,0:T(8,128)(2,1)S(1)}, bf16[4,24,1024]{2,1,0:T(8,128)(2,1)S(1)}, u32[]{:S(2)}, u32[]{:S(2)}) collective-permute-start(bf16[4,24,1024]{2,1,0:T(8,128)(2,1)S(1)} %shard_map.154.refs_0_), channel_id=1, source_target_pairs={{0,34},{1,35},{4,38},{5,39},{8,42},{9,43},{12,46},{13,47},{16,50},... | collective-permute-start | bytes 589832 | tf_op jit(solution)/shard_map/ppermute | solution.py:478
  122.1 0.8 collective-permute-start.27
  122.8 3.8 %collective-permute-done.29.refs_3_ = bf16[4,24,1024]{2,1,0:T(8,128)(2,1)S(1)} collective-permute-done((bf16[4,24,1024]{2,1,0:T(8,128)(2,1)S(1)}, bf16[4,24,1024]{2,1,0:T(8,128)(2,1)S(1)}, u32[]{:S(2)}, u32[]{:S(2)}) %collective-permute-start.29) | collective-permute-done | bytes 196640 | tf_op jit(solution)/shard_map/ppermute | solution.py:478
  126.6 1.3 collective-permute-done.28.refs_2_
  128.1 8.5 %collective-permute-start.30 = (bf16[4,4,24,1024]{3,2,1,0:T(8,128)(2,1)S(1)}, bf16[4,4,24,1024]{3,2,1,0:T(8,128)(2,1)S(1)}, u32[]{:S(2)}, u32[]{:S(2)}) collective-permute-start(bf16[4,4,24,1024]{3,2,1,0:T(8,128)(2,1)S(1)} %shard_map.155.own), channel_id=1, source_target_pairs={{0,1},{1,0},{4,5},{5,4},{8,9},{9,8},{12,13},{13,12},{16,17},{17,16... | collective-permute-start | bytes 2359304 | tf_op jit(solution)/shard_map/ppermute | solution.py:478
  136.6 1.9 %collective-permute-done.30.got = bf16[4,4,24,1024]{3,2,1,0:T(8,128)(2,1)S(1)} collective-permute-done((bf16[4,4,24,1024]{3,2,1,0:T(8,128)(2,1)S(1)}, bf16[4,4,24,1024]{3,2,1,0:T(8,128)(2,1)S(1)}, u32[]{:S(2)}, u32[]{:S(2)}) %collective-permute-start.30) | collective-permute-done | bytes 786464 | tf_op jit(solution)/shard_map/ppermute | solution.py:478
  138.5 1.4 shard_map.156
  (57 shorter events, 2.9 us)
Async XLA Ops:
  5.8 35.7 %all-to-all-start = ((bf16[8,8,128,128]{3,2,1,0:T(8,128)(2,1)}), bf16[8,8,128,128]{3,2,1,0:T(8,128)(2,1)S(1)}, u32[]{:S(2)}, u32[]{:S(2)}) async-start(bf16[8,8,128,128]{3,2,1,0:T(8,128)(2,1)} %shard_map.141), calls=%async_computation | async-start | bytes 4194304 | tf_op jit(solution)/shard_map/all_to_all | solution.py:583
  13.3 28.2 %copy-start.1 = (f32[3,128,128]{2,1,0:T(8,128)S(1)}, f32[3,128,128]{2,1,0:T(8,128)}, u32[]{:S(2)}) copy-start(f32[3,128,128]{2,1,0:T(8,128)} %constant.5.clone.within.refs_4_.refs_14_) | copy-start | bytes 589828
  13.3 28.2 %copy-start.2 = (bf16[3,32,3072]{2,1,0:T(8,128)(2,1)S(1)}, bf16[3,32,3072]{2,1,0:T(8,128)(2,1)}, u32[]{:S(2)}) copy-start(bf16[3,32,3072]{2,1,0:T(8,128)(2,1)} %refs_5_.1) | copy-start | bytes 1769476
  13.3 28.2 %copy-start.4 = (f32[3072]{0:T(1024)S(1)}, f32[3072]{0:T(1024)}, u32[]{:S(2)}) copy-start(f32[3072]{0:T(1024)} %param.18) | copy-start | bytes 36868
  13.3 28.2 %copy-start.9 = (s32[1,8]{1,0:T(1,128)S(1)}, s32[1,8]{1,0:T(1,128)}, u32[]{:S(2)}) copy-start(s32[1,8]{1,0:T(1,128)} %flags.5) | copy-start | bytes 100
  19.0 29.6 %collective-permute-start = (bf16[5,128,128]{2,1,0:T(8,128)(2,1)}, bf16[5,128,128]{2,1,0:T(8,128)(2,1)S(1)}, u32[]{:S(2)}, u32[]{:S(2)}) collective-permute-start(bf16[5,128,128]{2,1,0:T(8,128)(2,1)} %get-tuple-element.45), channel_id=1, source_target_pairs={{0,32},{1,33},{4,36},{5,37},{8,40},{9,41},{12,44},{13,45},{16,48},... | collective-permute-start | bytes 491528 | tf_op jit(solution)/shard_map/ppermute | solution.py:478
  22.1 26.6 %collective-permute-start.2 = (bf16[5,128,128]{2,1,0:T(8,128)(2,1)}, bf16[5,128,128]{2,1,0:T(8,128)(2,1)S(1)}, u32[]{:S(2)}, u32[]{:S(2)}) collective-permute-start(bf16[5,128,128]{2,1,0:T(8,128)(2,1)} %get-tuple-element.50), channel_id=1, source_target_pairs={{0,96},{1,97},{4,100},{5,101},{8,104},{9,105},{12,108},{13,109},{1... | collective-permute-start | bytes 491528 | tf_op jit(solution)/shard_map/ppermute | solution.py:478
  23.2 31.8 %collective-permute-start.3 = (bf16[5,128,128]{2,1,0:T(8,128)(2,1)}, bf16[5,128,128]{2,1,0:T(8,128)(2,1)S(1)}, u32[]{:S(2)}, u32[]{:S(2)}) collective-permute-start(bf16[5,128,128]{2,1,0:T(8,128)(2,1)} %get-tuple-element.51), channel_id=1, source_target_pairs={{0,128},{1,129},{4,132},{5,133},{8,136},{9,137},{12,140},{13,141},... | collective-permute-start | bytes 491528 | tf_op jit(solution)/shard_map/ppermute | solution.py:478
  25.6 29.4 %collective-permute-start.4 = (bf16[5,128,128]{2,1,0:T(8,128)(2,1)}, bf16[5,128,128]{2,1,0:T(8,128)(2,1)S(1)}, u32[]{:S(2)}, u32[]{:S(2)}) collective-permute-start(bf16[5,128,128]{2,1,0:T(8,128)(2,1)} %get-tuple-element.52), channel_id=1, source_target_pairs={{0,160},{1,161},{4,164},{5,165},{8,168},{9,169},{12,172},{13,173},... | collective-permute-start | bytes 491528 | tf_op jit(solution)/shard_map/ppermute | solution.py:478
  28.6 27.2 %collective-permute-start.6 = (bf16[5,128,128]{2,1,0:T(8,128)(2,1)}, bf16[5,128,128]{2,1,0:T(8,128)(2,1)}, u32[]{:S(2)}, u32[]{:S(2)}) collective-permute-start(bf16[5,128,128]{2,1,0:T(8,128)(2,1)} %get-tuple-element.54), channel_id=1, source_target_pairs={{0,224},{1,225},{4,228},{5,229},{8,232},{9,233},{12,236},{13,237},... | collective-permute-start | bytes 491528 | tf_op jit(solution)/shard_map/ppermute | solution.py:478
  41.6 0.7 copy-start.5
  42.3 0.7 copy-start.6
  43.0 5.6 %copy-start.11 = (bf16[5,128,128]{2,1,0:T(8,128)(2,1)S(1)}, bf16[5,128,128]{2,1,0:T(8,128)(2,1)}, u32[]{:S(2)}) copy-start(bf16[5,128,128]{2,1,0:T(8,128)(2,1)} %get-tuple-element.49) | copy-start | bytes 491524
  43.0 5.7 %copy-start.10 = (bf16[5,128,128]{2,1,0:T(8,128)(2,1)S(1)}, bf16[5,128,128]{2,1,0:T(8,128)(2,1)}, u32[]{:S(2)}) copy-start(bf16[5,128,128]{2,1,0:T(8,128)(2,1)} %get-tuple-element.53) | copy-start | bytes 491524
  48.6 12.2 %copy-start.3 = (bf16[5,128,128]{2,1,0:T(8,128)(2,1)S(1)}, bf16[5,128,128]{2,1,0:T(8,128)(2,1)}, u32[]{:S(2)}) copy-start(bf16[5,128,128]{2,1,0:T(8,128)(2,1)} %get-tuple-element.44.refs_0_) | copy-start | bytes 491524
  48.6 12.2 %copy-start.7 = (f32[24,128]{1,0:T(8,128)S(1)}, f32[24,128]{1,0:T(8,128)}, u32[]{:S(2)}) copy-start(f32[24,128]{1,0:T(8,128)} %constant.4.clone.by_frame.refs_3_.refs_10_.refs_13_) | copy-start | bytes 36868
  48.6 7.2 %collective-permute-start.1 = (bf16[5,128,128]{2,1,0:T(8,128)(2,1)S(1)}, bf16[5,128,128]{2,1,0:T(8,128)(2,1)S(1)}, u32[]{:S(2)}, u32[]{:S(2)}) collective-permute-start(bf16[5,128,128]{2,1,0:T(8,128)(2,1)S(1)} %copy-done.11), channel_id=1, source_target_pairs={{0,64},{1,65},{4,68},{5,69},{8,72},{9,73},{12,76},{13,77},{16,80},... | collective-permute-start | bytes 491528 | tf_op jit(solution)/shard_map/ppermute | solution.py:478
  48.7 12.0 %collective-permute-start.5 = (bf16[5,128,128]{2,1,0:T(8,128)(2,1)S(1)}, bf16[5,128,128]{2,1,0:T(8,128)(2,1)S(1)}, u32[]{:S(2)}, u32[]{:S(2)}) collective-permute-start(bf16[5,128,128]{2,1,0:T(8,128)(2,1)S(1)} %copy-done.10), channel_id=1, source_target_pairs={{0,192},{1,193},{4,196},{5,197},{8,200},{9,201},{12,204},{13,205},... | collective-permute-start | bytes 491528 | tf_op jit(solution)/shard_map/ppermute | solution.py:478
  60.8 17.2 %copy-start = (bf16[1,128,5120]{2,1,0:T(8,128)(2,1)S(1)}, bf16[1,128,5120]{2,1,0:T(8,128)(2,1)}, u32[]{:S(2)}) copy-start(bf16[1,128,5120]{2,1,0:T(8,128)(2,1)} %param.13) | copy-start | bytes 3932164
  60.8 17.2 %copy-start.8 = (f32[80,128]{1,0:T(8,128)S(1)}, f32[80,128]{1,0:T(8,128)}, u32[]{:S(2)}) copy-start(f32[80,128]{1,0:T(8,128)} %get-tuple-element.65.local) | copy-start | bytes 122884
  66.8 3.9 %collective-permute-start.7 = (bf16[224,128]{1,0:T(8,128)(2,1)S(1)}, bf16[224,128]{1,0:T(8,128)(2,1)S(1)}, u32[]{:S(2)}, u32[]{:S(2)}) collective-permute-start(bf16[224,128]{1,0:T(8,128)(2,1)S(1)} %get-tuple-element.59), channel_id=1, source_target_pairs={{0,64},{1,65},{4,68},{5,69},{8,72},{9,73},{12,76},{13,77},{16,80},... | collective-permute-start | bytes 172040 | tf_op jit(solution)/shard_map/ppermute | solution.py:478
  67.2 4.8 %collective-permute-start.8 = (bf16[224,128]{1,0:T(8,128)(2,1)S(1)}, bf16[224,128]{1,0:T(8,128)(2,1)S(1)}, u32[]{:S(2)}, u32[]{:S(2)}) collective-permute-start(bf16[224,128]{1,0:T(8,128)(2,1)S(1)} %get-tuple-element.60), channel_id=1, source_target_pairs={{0,128},{1,129},{4,132},{5,133},{8,136},{9,137},{12,140},{13,141},... | collective-permute-start | bytes 172040 | tf_op jit(solution)/shard_map/ppermute | solution.py:478
  68.9 4.7 %collective-permute-start.9 = (bf16[224,128]{1,0:T(8,128)(2,1)S(1)}, bf16[224,128]{1,0:T(8,128)(2,1)S(1)}, u32[]{:S(2)}, u32[]{:S(2)}) collective-permute-start(bf16[224,128]{1,0:T(8,128)(2,1)S(1)} %get-tuple-element.61), channel_id=1, source_target_pairs={{0,192},{1,193},{4,196},{5,197},{8,200},{9,201},{12,204},{13,205},... | collective-permute-start | bytes 172040 | tf_op jit(solution)/shard_map/ppermute | solution.py:478
  73.6 4.4 %collective-permute-start.10 = (bf16[128,128]{1,0:T(8,128)(2,1)S(1)}, bf16[128,128]{1,0:T(8,128)(2,1)S(1)}, u32[]{:S(2)}, u32[]{:S(2)}) collective-permute-start(bf16[128,128]{1,0:T(8,128)(2,1)S(1)} %get-tuple-element.64), channel_id=1, source_target_pairs={{0,32},{1,33},{4,36},{5,37},{8,40},{9,41},{12,44},{13,45},{16,48},... | collective-permute-start | bytes 98312 | tf_op jit(solution)/shard_map/ppermute | solution.py:478
  78.4 4.7 %collective-permute-start.11 = (bf16[4,4,24,640]{3,2,1,0:T(8,128)(2,1)S(1)}, bf16[4,4,24,640]{3,2,1,0:T(8,128)(2,1)S(1)}, u32[]{:S(2)}, u32[]{:S(2)}) collective-permute-start(bf16[4,4,24,640]{3,2,1,0:T(8,128)(2,1)S(1)} %get-tuple-element.67), channel_id=1, source_target_pairs={{0,1},{1,0},{4,5},{5,4},{8,9},{9,8},{12,13},{13,12},{16,17},{17,16... | collective-permute-start | bytes 1474568 | tf_op jit(solution)/shard_map/ppermute | solution.py:478
  83.2 8.0 %collective-permute-start.12 = (bf16[4,24,640]{2,1,0:T(8,128)(2,1)S(1)}, bf16[4,24,640]{2,1,0:T(8,128)(2,1)S(1)}, u32[]{:S(2)}, u32[]{:S(2)}) collective-permute-start(bf16[4,24,640]{2,1,0:T(8,128)(2,1)S(1)} %get-tuple-element.69), channel_id=1, source_target_pairs={{0,2},{1,3},{4,6},{5,7},{8,10},{9,11},{12,14},{13,15},{16,18},{17,... | collective-permute-start | bytes 368648 | tf_op jit(solution)/shard_map/ppermute | solution.py:478
  83.8 7.4 %collective-permute-start.13 = (bf16[4,24,640]{2,1,0:T(8,128)(2,1)S(1)}, bf16[4,24,640]{2,1,0:T(8,128)(2,1)S(1)}, u32[]{:S(2)}, u32[]{:S(2)}) collective-permute-start(bf16[4,24,640]{2,1,0:T(8,128)(2,1)S(1)} %get-tuple-element.70), channel_id=1, source_target_pairs={{0,32},{1,33},{4,36},{5,37},{8,40},{9,41},{12,44},{13,45},{16,48},... | collective-permute-start | bytes 368648 | tf_op jit(solution)/shard_map/ppermute | solution.py:478
  84.2 9.0 %collective-permute-start.14 = (bf16[4,24,640]{2,1,0:T(8,128)(2,1)S(1)}, bf16[4,24,640]{2,1,0:T(8,128)(2,1)S(1)}, u32[]{:S(2)}, u32[]{:S(2)}) collective-permute-start(bf16[4,24,640]{2,1,0:T(8,128)(2,1)S(1)} %get-tuple-element.71), channel_id=1, source_target_pairs={{0,34},{1,35},{4,38},{5,39},{8,42},{9,43},{12,46},{13,47},{16,50},... | collective-permute-start | bytes 368648 | tf_op jit(solution)/shard_map/ppermute | solution.py:478
  89.9 7.3 %collective-permute-start.18 = (bf16[2,24,384]{2,1,0:T(8,128)(2,1)S(1)}, bf16[2,24,384]{2,1,0:T(8,128)(2,1)S(1)}, u32[]{:S(2)}, u32[]{:S(2)}) collective-permute-start(bf16[2,24,384]{2,1,0:T(8,128)(2,1)S(1)} %get-tuple-element.81), channel_id=1, source_target_pairs={{0,1},{1,0},{4,5},{5,4},{8,9},{9,8},{12,13},{13,12},{16,17},{17,16... | collective-permute-start | bytes 110600 | tf_op jit(solution)/shard_map/ppermute | solution.py:478
  93.3 6.7 %collective-permute-start.15 = (bf16[24,640]{1,0:T(8,128)(2,1)S(1)}, bf16[24,640]{1,0:T(8,128)(2,1)S(1)}, u32[]{:S(2)}, u32[]{:S(2)}) collective-permute-start(bf16[24,640]{1,0:T(8,128)(2,1)S(1)} %get-tuple-element.73), channel_id=1, source_target_pairs={{0,64},{1,65},{4,68},{5,69},{8,72},{9,73},{12,76},{13,77},{16,80},... | collective-permute-start | bytes 92168 | tf_op jit(solution)/shard_map/ppermute | solution.py:478
  93.4 6.6 %collective-permute-start.16 = (bf16[24,640]{1,0:T(8,128)(2,1)S(1)}, bf16[24,640]{1,0:T(8,128)(2,1)S(1)}, u32[]{:S(2)}, u32[]{:S(2)}) collective-permute-start(bf16[24,640]{1,0:T(8,128)(2,1)S(1)} %get-tuple-element.74), channel_id=1, source_target_pairs={{0,128},{1,129},{4,132},{5,133},{8,136},{9,137},{12,140},{13,141},... | collective-permute-start | bytes 92168 | tf_op jit(solution)/shard_map/ppermute | solution.py:478
  96.3 4.0 %collective-permute-start.17 = (bf16[24,640]{1,0:T(8,128)(2,1)S(1)}, bf16[24,640]{1,0:T(8,128)(2,1)S(1)}, u32[]{:S(2)}, u32[]{:S(2)}) collective-permute-start(bf16[24,640]{1,0:T(8,128)(2,1)S(1)} %get-tuple-element.75), channel_id=1, source_target_pairs={{0,192},{1,193},{4,196},{5,197},{8,200},{9,201},{12,204},{13,205},... | collective-permute-start | bytes 92168 | tf_op jit(solution)/shard_map/ppermute | solution.py:478
  97.2 2.7 %collective-permute-start.19 = (bf16[24,384]{1,0:T(8,128)(2,1)S(1)}, bf16[24,384]{1,0:T(8,128)(2,1)S(1)}, u32[]{:S(2)}, u32[]{:S(2)}) collective-permute-start(bf16[24,384]{1,0:T(8,128)(2,1)S(1)} %get-tuple-element.83), channel_id=1, source_target_pairs={{0,2},{1,3},{4,6},{5,7},{8,10},{9,11},{12,14},{13,15},{16,18},{17,... | collective-permute-start | bytes 55304 | tf_op jit(solution)/shard_map/ppermute | solution.py:478
  100.3 5.9 %collective-permute-start.22 = (bf16[24,1024]{1,0:T(8,128)(2,1)S(1)}, bf16[24,1024]{1,0:T(8,128)(2,1)S(1)}, u32[]{:S(2)}, u32[]{:S(2)}) collective-permute-start(bf16[24,1024]{1,0:T(8,128)(2,1)S(1)} %shard_map.151.own), channel_id=1, source_target_pairs={{0,12},{1,13},{4,8},{5,9},{8,4},{9,5},{12,0},{13,1},{16,28},{17,29... | collective-permute-start | bytes 147464 | tf_op jit(solution)/shard_map/ppermute | solution.py:478
  104.8 4.4 %collective-permute-start.21 = (bf16[24,1024]{1,0:T(8,128)(2,1)S(1)}, bf16[24,1024]{1,0:T(8,128)(2,1)S(1)}, u32[]{:S(2)}, u32[]{:S(2)}) collective-permute-start(bf16[24,1024]{1,0:T(8,128)(2,1)S(1)} %shard_map.151.own), channel_id=1, source_target_pairs={{0,8},{1,9},{4,12},{5,13},{8,0},{9,1},{12,4},{13,5},{16,24},{17,25... | collective-permute-start | bytes 147464 | tf_op jit(solution)/shard_map/ppermute | solution.py:478
  104.8 4.4 %collective-permute-start.20 = (bf16[24,1024]{1,0:T(8,128)(2,1)S(1)}, bf16[24,1024]{1,0:T(8,128)(2,1)S(1)}, u32[]{:S(2)}, u32[]{:S(2)}) collective-permute-start(bf16[24,1024]{1,0:T(8,128)(2,1)S(1)} %shard_map.151.own), channel_id=1, source_target_pairs={{0,4},{1,5},{4,0},{5,1},{8,12},{9,13},{12,8},{13,9},{16,20},{17,21... | collective-permute-start | bytes 147464 | tf_op jit(solution)/shard_map/ppermute | solution.py:478
  109.2 4.6 %collective-permute-start.23 = (bf16[24,1024]{1,0:T(8,128)(2,1)S(1)}, bf16[24,1024]{1,0:T(8,128)(2,1)S(1)}, u32[]{:S(2)}, u32[]{:S(2)}) collective-permute-start(bf16[24,1024]{1,0:T(8,128)(2,1)S(1)} %shard_map.152.own), channel_id=1, source_target_pairs={{0,28},{1,29},{4,24},{5,25},{8,20},{9,21},{12,16},{13,17},{16,12},... | collective-permute-start | bytes 147464 | tf_op jit(solution)/shard_map/ppermute | solution.py:478
  113.7 4.2 %collective-permute-start.26 = (bf16[24,1024]{1,0:T(8,128)(2,1)S(1)}, bf16[24,1024]{1,0:T(8,128)(2,1)S(1)}, u32[]{:S(2)}, u32[]{:S(2)}) collective-permute-start(bf16[24,1024]{1,0:T(8,128)(2,1)S(1)} %shard_map.153.refs_0_), channel_id=1, source_target_pairs={{0,192},{1,193},{4,196},{5,197},{8,200},{9,201},{12,204},{13,205},... | collective-permute-start | bytes 147464 | tf_op jit(solution)/shard_map/ppermute | solution.py:478
  115.0 4.4 %collective-permute-start.25 = (bf16[24,1024]{1,0:T(8,128)(2,1)S(1)}, bf16[24,1024]{1,0:T(8,128)(2,1)S(1)}, u32[]{:S(2)}, u32[]{:S(2)}) collective-permute-start(bf16[24,1024]{1,0:T(8,128)(2,1)S(1)} %shard_map.153.refs_0_), channel_id=1, source_target_pairs={{0,128},{1,129},{4,132},{5,133},{8,136},{9,137},{12,140},{13,141},... | collective-permute-start | bytes 147464 | tf_op jit(solution)/shard_map/ppermute | solution.py:478
  115.0 4.4 %collective-permute-start.24 = (bf16[24,1024]{1,0:T(8,128)(2,1)S(1)}, bf16[24,1024]{1,0:T(8,128)(2,1)S(1)}, u32[]{:S(2)}, u32[]{:S(2)}) collective-permute-start(bf16[24,1024]{1,0:T(8,128)(2,1)S(1)} %shard_map.153.refs_0_), channel_id=1, source_target_pairs={{0,64},{1,65},{4,68},{5,69},{8,72},{9,73},{12,76},{13,77},{16,80},... | collective-permute-start | bytes 147464 | tf_op jit(solution)/shard_map/ppermute | solution.py:478
  119.5 7.2 %collective-permute-start.29 = (bf16[4,24,1024]{2,1,0:T(8,128)(2,1)S(1)}, bf16[4,24,1024]{2,1,0:T(8,128)(2,1)S(1)}, u32[]{:S(2)}, u32[]{:S(2)}) collective-permute-start(bf16[4,24,1024]{2,1,0:T(8,128)(2,1)S(1)} %shard_map.154.refs_0_), channel_id=1, source_target_pairs={{0,34},{1,35},{4,38},{5,39},{8,42},{9,43},{12,46},{13,47},{16,50},... | collective-permute-start | bytes 589832 | tf_op jit(solution)/shard_map/ppermute | solution.py:478
  121.9 6.0 %collective-permute-start.28 = (bf16[4,24,1024]{2,1,0:T(8,128)(2,1)S(1)}, bf16[4,24,1024]{2,1,0:T(8,128)(2,1)S(1)}, u32[]{:S(2)}, u32[]{:S(2)}) collective-permute-start(bf16[4,24,1024]{2,1,0:T(8,128)(2,1)S(1)} %shard_map.154.refs_0_), channel_id=1, source_target_pairs={{0,32},{1,33},{4,36},{5,37},{8,40},{9,41},{12,44},{13,45},{16,48},... | collective-permute-start | bytes 589832 | tf_op jit(solution)/shard_map/ppermute | solution.py:478
  122.1 6.0 %collective-permute-start.27 = (bf16[4,24,1024]{2,1,0:T(8,128)(2,1)S(1)}, bf16[4,24,1024]{2,1,0:T(8,128)(2,1)S(1)}, u32[]{:S(2)}, u32[]{:S(2)}) collective-permute-start(bf16[4,24,1024]{2,1,0:T(8,128)(2,1)S(1)} %shard_map.154.refs_0_), channel_id=1, source_target_pairs={{0,2},{1,3},{4,6},{5,7},{8,10},{9,11},{12,14},{13,15},{16,18},{17,... | collective-permute-start | bytes 589832 | tf_op jit(solution)/shard_map/ppermute | solution.py:478
  128.1 10.4 %collective-permute-start.30 = (bf16[4,4,24,1024]{3,2,1,0:T(8,128)(2,1)S(1)}, bf16[4,4,24,1024]{3,2,1,0:T(8,128)(2,1)S(1)}, u32[]{:S(2)}, u32[]{:S(2)}) collective-permute-start(bf16[4,4,24,1024]{3,2,1,0:T(8,128)(2,1)S(1)} %shard_map.155.own), channel_id=1, source_target_pairs={{0,1},{1,0},{4,5},{5,4},{8,9},{9,8},{12,13},{13,12},{16,17},{17,16... | collective-permute-start | bytes 2359304 | tf_op jit(solution)/shard_map/ppermute | solution.py:478
